TPU v7x, 512 devices: a whole 4x4x16 slice. The times are simulated.
512 devices in a mesh: dp: 512 (over y, x, z, core).
Axes of the slice: x: 4, y: 4, z: 16, core: 2. Of those that a mesh axis runs over, the one named last changes fastest.
Arguments:
- picture_embedding: float32 [196608, 768], P('dp'), may hold values from -0.3 to 0.3
- caption_embedding: float32 [196608, 768], P('dp'), may hold values from -0.3 to 0.3
- match_class_tags: int32 [196608], P('dp'), may hold values from 0 to 49151
- natural_log_heat: float32 [1], replicated, may hold values from 1.5 to 2.5
- offset_term: float32 [1], replicated, may hold values from -3 to -1
Outputs:
- picture_sensitivity: float32 [196608, 768], P('dp')
- caption_sensitivity: float32 [196608, 768], P('dp')
All inputs are finite; a program needn't handle non-finite values.
Results may differ from a plain program's by a relative error of at most 0.0003.
Values sent between devices are 32-bit elements; how exact they have to be, the bound alone decides.
No kernel may reach another device: no remote copies, remote signals or barrier semaphores. Data moves between devices by JAX's collectives and lax.ppermute only.
A program may use at most 64 MiB of HBM per device.

v0:
```python
import jax
import jax.numpy as jnp
from jax import lax
from jax.sharding import PartitionSpec as P


def from_behind(block, axis, distance):
    devices = range(lax.axis_size(axis))
    route = [((i - distance) % len(devices), i) for i in devices]
    return lax.ppermute(block, axis, route)


def normalize(rows):
    return rows * lax.rsqrt(jnp.sum(rows * rows, axis=-1, keepdims=True) + 1e-06)


def tile_slopes(
    former_peer,
    latter_peer,
    former_class_tags,
    latter_class_tags,
    sharpness_factor,
    tile_shift_amount,
):
    similarity_matrix = (
        sharpness_factor
        * jnp.dot(
            former_peer,
            latter_peer.T,
            precision=lax.Precision.HIGHEST,
            preferred_element_type=jnp.float32,
        )
        + tile_shift_amount
    )
    labels = jnp.where(former_class_tags[:, None] == latter_class_tags[None, :], 1.0, -1.0).astype(
        jnp.float32
    )
    return -labels * jax.nn.sigmoid(-labels * similarity_matrix)


def product(former_peer, latter_peer):
    return jnp.dot(
        former_peer,
        latter_peer,
        precision=lax.Precision.HIGHEST,
        preferred_element_type=jnp.float32,
    )


def local(picture_embedding, caption_embedding, match_class_tags, natural_log_heat, offset_term):
    sharpness_factor = jnp.exp(natural_log_heat[0])
    tile_shift_amount = offset_term[0]
    unit_image_rows, incoming_picture = jax.vjp(normalize, picture_embedding)
    unit_text_rows, incoming_caption = jax.vjp(normalize, caption_embedding)
    similarity_slopes = tile_slopes(
        unit_image_rows,
        unit_text_rows,
        match_class_tags,
        match_class_tags,
        sharpness_factor,
        tile_shift_amount,
    )
    picture_pull = product(similarity_slopes, unit_text_rows)
    caption_pull = product(similarity_slopes.T, unit_image_rows)
    group_size = lax.axis_size("dp")
    for shift_by in (1, group_size // 2):
        distant_text, distant_label_ids = from_behind(
            (unit_text_rows, match_class_tags), "dp", shift_by
        )
        similarity_slopes = tile_slopes(
            unit_image_rows,
            distant_text,
            match_class_tags,
            distant_label_ids,
            sharpness_factor,
            tile_shift_amount,
        )
        picture_pull = picture_pull + product(similarity_slopes, distant_text)
        partial_pull = product(similarity_slopes.T, unit_image_rows)
        caption_pull = caption_pull + from_behind(partial_pull, "dp", group_size - shift_by)
    picture_sensitivity = incoming_picture(sharpness_factor * picture_pull)[0]
    caption_sensitivity = incoming_caption(sharpness_factor * caption_pull)[0]
    return (picture_sensitivity, caption_sensitivity)


def solution(mesh):
    return jax.shard_map(
        local,
        mesh=mesh,
        in_specs=(P("dp", None), P("dp", None), P("dp"), P(), P()),
        out_specs=(P("dp", None), P("dp", None)),
        check_vma=False,
    )
```

profile of v0, /device:TPU:494, one launch (start us, length us, event | category | flops | bytes accessed | tf_op | source)
XLA Modules:
  0.0 87.2 jit_solution(3953811612244790128)
XLA Ops:
  0.6 1.5 %multiply_reduce_fusion.2 = f32[384]{0:T(512)S(1)} fusion(f32[384,768]{1,0:T(8,128)} %param.6), kind=kLoop, calls=%fused_computation.34 | loop fusion | flops 589440 | bytes 1181184 | tf_op jit(solution)/shard_map/jvp()/reduce_sum | solution.py:14
  2.2 0.1 copy-done.1
  2.3 0.1 broadcast_multiply_fusion
  2.4 4.3 %collective-permute-start.3 = (f32[384,768]{1,0:T(8,128)S(1)}, f32[384,768]{1,0:T(8,128)S(1)}, u32[]{:S(2)}, u32[]{:S(2)}) collective-permute-start(f32[384,768]{1,0:T(8,128)S(1)} %broadcast_multiply_fusion), channel_id=1, source_target_pairs={{256,0},{257,1},{258,2},{259,3},{260,4},{261,5},{262,6},{263,7},{2... | collective-permute-start | bytes 3538952 | tf_op jit(solution)/shard_map/ppermute | solution.py:10
  6.8 1.9 %collective-permute-start.1 = (f32[384,768]{1,0:T(8,128)S(1)}, f32[384,768]{1,0:T(8,128)S(1)}, u32[]{:S(2)}, u32[]{:S(2)}) collective-permute-start(f32[384,768]{1,0:T(8,128)S(1)} %broadcast_multiply_fusion), channel_id=1, source_target_pairs={{511,0},{0,1},{1,2},{2,3},{3,4},{4,5},{5,6},{6,7},{7,8},{8,9},{9,1... | collective-permute-start | bytes 3538952 | tf_op jit(solution)/shard_map/ppermute | solution.py:10
  8.7 1.9 %collective-permute-start = (s32[384]{0:T(512)S(1)}, s32[384]{0:T(512)S(1)}, u32[]{:S(2)}, u32[]{:S(2)}) collective-permute-start(s32[384]{0:T(512)S(1)} %copy-done.2), channel_id=1, source_target_pairs={{511,0},{0,1},{1,2},{2,3},{3,4},{4,5},{5,6},{6,7},{7,8},{8,9},{9,1... | collective-permute-start | bytes 4616 | tf_op jit(solution)/shard_map/ppermute | solution.py:10
  10.6 3.1 %collective-permute-start.2 = (s32[384]{0:T(512)S(1)}, s32[384]{0:T(512)S(1)}, u32[]{:S(2)}, u32[]{:S(2)}) collective-permute-start(s32[384]{0:T(512)S(1)} %copy-done.2), channel_id=1, source_target_pairs={{256,0},{257,1},{258,2},{259,3},{260,4},{261,5},{262,6},{263,7},{2... | collective-permute-start | bytes 4616 | tf_op jit(solution)/shard_map/ppermute | solution.py:10
  15.1 0.2 multiply_reduce_fusion.3
  15.3 2.3 %fusion.17 = f32[384,384]{1,0:T(8,128)S(1)} fusion(f32[384,768]{1,0:T(8,128)S(1)} %broadcast_multiply_fusion, f32[384,768]{1,0:T(8,128)S(1)} %copy-done, f32[384]{0:T(512)S(1)} %add_rsqrt_fusion.1, f32[]{:T(128)} %bitcast.14, f32[]{:T(128)} %bitcast, s32[384]{0:T(512)S(1)} %copy-done.2), kind=kOutput, calls=%fused_computation.25 | convolution fusion | flops 1360723968 | bytes 2952200 | tf_op jit(solution)/shard_map/dot_general | solution.py:27
  17.6 2.1 %fusion.38 = f32[384,768]{1,0:T(8,128)S(1)} fusion(f32[384,384]{1,0:T(8,128)S(1)} %fusion.17, f32[384,768]{1,0:T(8,128)S(1)} %broadcast_multiply_fusion), kind=kOutput, calls=%fused_computation.55 | convolution fusion | flops 1358954496 | bytes 2949120 | tf_op jit(solution)/shard_map/dot_general | solution.py:42
  19.7 14.0 %collective-permute-done.2 = s32[384]{0:T(512)S(1)} collective-permute-done((s32[384]{0:T(512)S(1)}, s32[384]{0:T(512)S(1)}, u32[]{:S(2)}, u32[]{:S(2)}) %collective-permute-start.2) | collective-permute-done | bytes 1568 | tf_op jit(solution)/shard_map/ppermute | solution.py:10
  33.7 0.0 collective-permute-done.3
  33.7 2.3 %fusion.23 = f32[384,384]{1,0:T(8,128)S(1)} fusion(f32[384,768]{1,0:T(8,128)S(1)} %collective-permute-done.3, f32[384,768]{1,0:T(8,128)S(1)} %copy-done, f32[384]{0:T(512)S(1)} %add_rsqrt_fusion.1, s32[384]{0:T(512)S(1)} %collective-permute-done.2, f32[]{:T(128)} %bitcast.15, f32[]{:T(128)} %bitcast, s32[384]{0:T(512)S(1)} %copy-done.2), kind=kOutput, calls=%fused_computation.31 | convolution fusion | flops 1360723968 | bytes 2953736 | tf_op jit(solution)/shard_map/dot_general | solution.py:27
  36.0 2.3 %fusion.24 = f32[384,768]{1,0:T(8,128)S(1)} fusion(f32[384,384]{1,0:T(8,128)S(1)} %fusion.23, f32[384,768]{1,0:T(8,128)S(1)} %copy-done, f32[384]{0:T(512)S(1)} %add_rsqrt_fusion.1), kind=kOutput, calls=%fused_computation.36 | convolution fusion | flops 1359249408 | bytes 2950656 | tf_op jit(solution)/shard_map/dot_general | solution.py:42
  38.3 4.4 %collective-permute-start.5 = (f32[384,768]{1,0:T(8,128)S(1)}, f32[384,768]{1,0:T(8,128)S(1)}, u32[]{:S(2)}, u32[]{:S(2)}) collective-permute-start(f32[384,768]{1,0:T(8,128)S(1)} %fusion.24), channel_id=1, source_target_pairs={{256,0},{257,1},{258,2},{259,3},{260,4},{261,5},{262,6},{263,7},{2... | collective-permute-start | bytes 3538952 | tf_op jit(solution)/shard_map/ppermute | solution.py:10
  42.7 2.3 %fusion.20 = f32[384,384]{1,0:T(8,128)S(1)} fusion(f32[384,768]{1,0:T(8,128)S(1)} %collective-permute-done.1, f32[384,768]{1,0:T(8,128)S(1)} %copy-done, f32[384]{0:T(512)S(1)} %add_rsqrt_fusion.1, s32[384]{0:T(512)S(1)} %collective-permute-done, f32[]{:T(128)} %bitcast.16, f32[]{:T(128)} %bitcast, s32[384]{0:T(512)S(1)} %copy-done.2), kind=kOutput, calls=%fused_computation.28 | convolution fusion | flops 1360723968 | bytes 2953736 | tf_op jit(solution)/shard_map/dot_general | solution.py:27
  45.0 2.2 %fusion.26 = f32[384,768]{1,0:T(8,128)S(1)} fusion(f32[384,384]{1,0:T(8,128)S(1)} %fusion.20, f32[384,768]{1,0:T(8,128)S(1)} %copy-done, f32[384]{0:T(512)S(1)} %add_rsqrt_fusion.1), kind=kOutput, calls=%fused_computation.38 | convolution fusion | flops 1359249408 | bytes 2950656 | tf_op jit(solution)/shard_map/dot_general | solution.py:42
  47.2 1.9 %collective-permute-start.4 = (f32[384,768]{1,0:T(8,128)S(1)}, f32[384,768]{1,0:T(8,128)S(1)}, u32[]{:S(2)}, u32[]{:S(2)}) collective-permute-start(f32[384,768]{1,0:T(8,128)S(1)} %fusion.26), channel_id=1, source_target_pairs={{1,0},{2,1},{3,2},{4,3},{5,4},{6,5},{7,6},{8,7},{9,8},{10,9},{11,1... | collective-permute-start | bytes 3538952 | tf_op jit(solution)/shard_map/ppermute | solution.py:10
  49.1 2.1 %convolution_add_fusion.2 = f32[384,768]{1,0:T(8,128)S(1)} fusion(f32[384,768]{1,0:T(8,128)S(1)} %fusion.38, f32[384,384]{1,0:T(8,128)S(1)} %fusion.20, f32[384,768]{1,0:T(8,128)S(1)} %collective-permute-done.1), kind=kOutput, calls=%fused_computation.7 | convolution fusion | flops 1359249408 | bytes 4128768 | tf_op jit(solution)/shard_map/dot_general | solution.py:42
  51.2 2.3 %multiply_reduce_fusion.1 = (f32[384]{0:T(512)S(1)}, f32[384,768]{1,0:T(8,128)S(1)}) fusion(f32[384,768]{1,0:T(8,128)S(1)} %copy-done, f32[384,768]{1,0:T(8,128)S(1)} %convolution_add_fusion.2, f32[384,384]{1,0:T(8,128)S(1)} %fusion.23, f32[384,768]{1,0:T(8,128)S(1)} %collective-permute-done.3, f32[]{:T(128)} %bitcast), kind=kOutput, calls=%fused_computation.33 | convolution fusion | flops 1360133760 | bytes 5309956 | tf_op jit(solution)/shard_map/dot_general | solution.py:42
  53.6 1.3 %add_add_fusion.1 = f32[384,768]{1,0:T(8,128)} fusion(f32[384,768]{1,0:T(8,128)S(1)} %copy-done, f32[384,768]{1,0:T(8,128)S(1)} %get-tuple-element.3, f32[384]{0:T(512)S(1)} %multiply_multiply_fusion.1, f32[384]{0:T(512)S(1)} %add_rsqrt_fusion.1), kind=kLoop, calls=%fused_computation.1 | loop fusion | flops 1179648 | bytes 3542016 | tf_op jit(solution)/shard_map/transpose(jvp())/add_any | solution.py:14
  54.8 28.6 %collective-permute-done.5 = f32[384,768]{1,0:T(8,128)S(1)} collective-permute-done((f32[384,768]{1,0:T(8,128)S(1)}, f32[384,768]{1,0:T(8,128)S(1)}, u32[]{:S(2)}, u32[]{:S(2)}) %collective-permute-start.5) | collective-permute-done | bytes 1179680 | tf_op jit(solution)/shard_map/ppermute | solution.py:10
  83.4 2.5 %multiply_reduce_fusion = (f32[384]{0:T(512)S(1)}, f32[384,768]{1,0:T(8,128)S(1)}) fusion(f32[384,768]{1,0:T(8,128)S(1)} %copy-done.1, f32[384,768]{1,0:T(8,128)S(1)} %collective-permute-done.5, f32[384,768]{1,0:T(8,128)S(1)} %collective-permute-done.4, f32[384,384]{1,0:T(8,128)S(1)} %fusion.17, f32[384,768]{1,0:T(8,128)S(1)} %copy-done, ...), kind=kOutput, calls=%fused_computation.32 | convolution fusion | flops 1360723584 | bytes 6491140 | tf_op jit(solution)/shard_map/dot_general | solution.py:42
  85.9 1.3 %add_add_fusion = f32[384,768]{1,0:T(8,128)} fusion(f32[384,768]{1,0:T(8,128)S(1)} %copy-done.1, f32[384,768]{1,0:T(8,128)S(1)} %get-tuple-element.5, f32[384]{0:T(512)S(1)} %multiply_multiply_fusion, f32[384]{0:T(512)S(1)} %add_rsqrt_fusion), kind=kLoop, calls=%fused_computation | loop fusion | flops 1179648 | bytes 3542016 | tf_op jit(solution)/shard_map/transpose(jvp())/add_any | solution.py:14
  (12 shorter events, 0.1 us)
Async XLA Ops:
  0.6 1.6 %copy-start.1 = (f32[384,768]{1,0:T(8,128)S(1)}, f32[384,768]{1,0:T(8,128)}, u32[]{:S(2)}) copy-start(f32[384,768]{1,0:T(8,128)} %param.6) | copy-start | bytes 3538948
  2.3 6.4 %copy-start.2 = (s32[384]{0:T(512)S(1)}, s32[384]{0:T(512)}, u32[]{:S(2)}) copy-start(s32[384]{0:T(512)} %param.7) | copy-start | bytes 4612
  2.3 12.8 %copy-start = (f32[384,768]{1,0:T(8,128)S(1)}, f32[384,768]{1,0:T(8,128)}, u32[]{:S(2)}) copy-start(f32[384,768]{1,0:T(8,128)} %param.5) | copy-start | bytes 3538948
  2.4 31.3 %collective-permute-start.3 = (f32[384,768]{1,0:T(8,128)S(1)}, f32[384,768]{1,0:T(8,128)S(1)}, u32[]{:S(2)}, u32[]{:S(2)}) collective-permute-start(f32[384,768]{1,0:T(8,128)S(1)} %broadcast_multiply_fusion), channel_id=1, source_target_pairs={{256,0},{257,1},{258,2},{259,3},{260,4},{261,5},{262,6},{263,7},{2... | collective-permute-start | bytes 3538952 | tf_op jit(solution)/shard_map/ppermute | solution.py:10
  6.8 35.9 %collective-permute-start.1 = (f32[384,768]{1,0:T(8,128)S(1)}, f32[384,768]{1,0:T(8,128)S(1)}, u32[]{:S(2)}, u32[]{:S(2)}) collective-permute-start(f32[384,768]{1,0:T(8,128)S(1)} %broadcast_multiply_fusion), channel_id=1, source_target_pairs={{511,0},{0,1},{1,2},{2,3},{3,4},{4,5},{5,6},{6,7},{7,8},{8,9},{9,1... | collective-permute-start | bytes 3538952 | tf_op jit(solution)/shard_map/ppermute | solution.py:10
  8.7 34.0 %collective-permute-start = (s32[384]{0:T(512)S(1)}, s32[384]{0:T(512)S(1)}, u32[]{:S(2)}, u32[]{:S(2)}) collective-permute-start(s32[384]{0:T(512)S(1)} %copy-done.2), channel_id=1, source_target_pairs={{511,0},{0,1},{1,2},{2,3},{3,4},{4,5},{5,6},{6,7},{7,8},{8,9},{9,1... | collective-permute-start | bytes 4616 | tf_op jit(solution)/shard_map/ppermute | solution.py:10
  10.6 23.1 %collective-permute-start.2 = (s32[384]{0:T(512)S(1)}, s32[384]{0:T(512)S(1)}, u32[]{:S(2)}, u32[]{:S(2)}) collective-permute-start(s32[384]{0:T(512)S(1)} %copy-done.2), channel_id=1, source_target_pairs={{256,0},{257,1},{258,2},{259,3},{260,4},{261,5},{262,6},{263,7},{2... | collective-permute-start | bytes 4616 | tf_op jit(solution)/shard_map/ppermute | solution.py:10
  38.3 45.1 %collective-permute-start.5 = (f32[384,768]{1,0:T(8,128)S(1)}, f32[384,768]{1,0:T(8,128)S(1)}, u32[]{:S(2)}, u32[]{:S(2)}) collective-permute-start(f32[384,768]{1,0:T(8,128)S(1)} %fusion.24), channel_id=1, source_target_pairs={{256,0},{257,1},{258,2},{259,3},{260,4},{261,5},{262,6},{263,7},{2... | collective-permute-start | bytes 3538952 | tf_op jit(solution)/shard_map/ppermute | solution.py:10
  47.2 36.2 %collective-permute-start.4 = (f32[384,768]{1,0:T(8,128)S(1)}, f32[384,768]{1,0:T(8,128)S(1)}, u32[]{:S(2)}, u32[]{:S(2)}) collective-permute-start(f32[384,768]{1,0:T(8,128)S(1)} %fusion.26), channel_id=1, source_target_pairs={{1,0},{2,1},{3,2},{4,3},{5,4},{6,5},{7,6},{8,7},{9,8},{10,9},{11,1... | collective-permute-start | bytes 3538952 | tf_op jit(solution)/shard_map/ppermute | solution.py:10
where the time goes:
time: 87.5 us; the launch traced here: 87.2 us
  waiting for transfers between devices  42.6 us (49%)
  matrix products  20.4 us (23%)
  starting transfers between devices  17.6 us (20%)
  other arithmetic  4.39 us (5%)
  between operations  2.12 us (2%)
    ppermute x6, waiting for transfers between devices, from_behind(): return lax.ppermute(block, axis, route)  42.6 us
    ppermute x6, starting transfers between devices, from_behind(): return lax.ppermute(block, axis, route)  17.6 us
    dot_general x6, matrix products, product(): jnp.dot(former_peer, latter_peer, precision=lax.Precision.HIGHEST, prefer...  13.5 us
    dot_general x3, matrix products, tile_slopes(): jnp.dot(former_peer, latter_peer.T, precision=lax.Precision.HIGHEST, pref...  6.83 us
    add_any x2, other arithmetic, normalize(): rows * rows  2.53 us
  transfers between devices with their start and end apart: 6, of which 2 were waited for; matrix products, arithmetic and copies ran while one was open for 22% of the time, Pallas kernels for 0%

commit v1 on v0

v1 whole, which is shorter than its diff:
```python
import functools

import jax
import jax.numpy as jnp
from jax import lax
from jax.experimental import pallas as pl
from jax.experimental.pallas import tpu as pltpu
from jax.sharding import PartitionSpec as P

NT = (((1,), (1,)), ((), ()))
NN = (((1,), (0,)), ((), ()))
PLANE = 128
DEEP = 16
RELAYS = ((0, 15), (3, 0))
PARTS = len(RELAYS) + 1
VMEM = pl.BlockSpec(memory_space=pltpu.VMEM)
SMEM = pl.BlockSpec(memory_space=pltpu.SMEM)


def shift(block, distance, skip=False):
    count = lax.axis_size("dp")
    route = [(i, (i + distance) % count) for i in range(count)]
    if skip:
        route = [(i, j) for i, j in route if i // PLANE == j // PLANE]
    return lax.ppermute(block, "dp", route)


def relay(column, core):
    return (column[0] * DEEP + column[1]) * 2 + core


def outward(block, column):
    count = lax.axis_size("dp")
    up = 0 if column is None else relay(column, 0)
    down = PLANE - 1 if column is None else relay(column, 1)
    route = []
    for plane in range(0, count, PLANE):
        route.append((plane + PLANE - 1, (plane + PLANE) % count + up))
        route.append((plane, (plane - PLANE) % count + down))
    return lax.ppermute(block, "dp", route)


def homeward(block, column):
    count = lax.axis_size("dp")
    route = []
    for plane in range(0, count, PLANE):
        route.append((plane + relay(column, 0), plane))
        route.append((plane + relay(column, 1), plane + PLANE - 1))
    return lax.ppermute(block, "dp", route)


def inverse_norm(rows):
    return lax.rsqrt(jnp.sum(rows * rows, axis=-1, keepdims=True) + 1e-06)


def halves(value):
    high = value.astype(jnp.bfloat16)
    low = (value - high.astype(jnp.float32)).astype(jnp.bfloat16)
    return high, low


def dot3(left, right, dims):
    dot = functools.partial(lax.dot_general, dimension_numbers=dims, preferred_element_type=jnp.float32)
    return dot(left[0], right[0]) + (dot(left[0], right[1]) + dot(left[1], right[0]))


def column_of(row):
    return jnp.transpose(jnp.broadcast_to(row, (8, row.shape[1])))[:, :1]


def slopes(own, other, own_tags, other_tags, heat, bias):
    logit = heat * dot3(own, other, NT) + bias
    same = own_tags == other_tags
    slope = 1.0 / (1.0 + jnp.exp(jnp.where(same, logit, -logit)))
    return jnp.where(same, -slope, slope)


def pull(own, other, *tags_and_scalars):
    return dot3(halves(slopes(own, other, *tags_and_scalars)), other, NN)


def scalars(heat_ref, bias_ref):
    return jnp.exp(jnp.full((1, 1), heat_ref[0], jnp.float32)), bias_ref[0]


def through_norm(total, unit, scale, heat):
    total = heat * total
    return scale * (total - unit * jnp.sum(unit * total, axis=-1, keepdims=True))


def put_tags(ref, tags):
    count = ref.shape[0] - 8
    ref[count:, :] = jnp.zeros((8, ref.shape[1]), jnp.float32)
    ref[count : count + 1, : tags.shape[1]] = tags


def unit_kernel(
    caption_ref, picture_ref, tags_ref,
    caption_out, picture_out, caption_scale, picture_scale, *refs,
):
    parts, (raw, sem) = refs[:PARTS], refs[PARTS:]
    rows = tags_ref.shape[1]
    first = pltpu.make_async_copy(caption_ref, raw.at[0], sem.at[0])
    second = pltpu.make_async_copy(picture_ref, raw.at[1], sem.at[1])
    first.start()
    second.start()
    tags = tags_ref[...].astype(jnp.float32)
    place = lax.rem(lax.axis_index("dp"), PLANE)
    for k, (copy, out, scale_out) in enumerate(
        ((first, caption_out, caption_scale), (second, picture_out, picture_scale))
    ):
        copy.wait()
        value = raw[k]
        scale = inverse_norm(value)
        out[:rows, :] = value * scale
        put_tags(out, tags)
        scale_out[...] = jnp.broadcast_to(scale, scale_out.shape)

    def cut(source):
        step = rows // PARTS
        for k, part in enumerate(parts):
            part[:step, :] = source[k * step : (k + 1) * step, :]
        put_tags(parts[0], tags)

    @pl.when(place == PLANE - 1)
    def _():
        cut(caption_out)

    @pl.when(place == 0)
    def _():
        cut(picture_out)


def own_kernel(
    heat_ref, bias_ref, caption_ref, picture_ref,
    picture_high_ref, picture_low_ref, caption_high_ref, caption_low_ref, p_ref, c_ref,
):
    heat, bias = scalars(heat_ref, bias_ref)
    rows = p_ref.shape[0]
    tags = caption_ref[rows : rows + 1, :rows]
    picture, caption = halves(picture_ref[:rows, :]), halves(caption_ref[:rows, :])
    picture_high_ref[...], picture_low_ref[...] = picture
    caption_high_ref[...], caption_low_ref[...] = caption
    slope = slopes(picture, caption, column_of(tags), tags, heat, bias)
    p_ref[...] = dot3(halves(slope), caption, NN)
    c_ref[...] = dot3(halves(jnp.transpose(slope)), picture, NN)


def far_caption_kernel(heat_ref, bias_ref, own_ref, high_ref, low_ref, far_ref, in_ref, out_ref):
    heat, bias = scalars(heat_ref, bias_ref)
    rows = out_ref.shape[0]
    own_tags = column_of(own_ref[rows : rows + 1, :rows])
    tags = far_ref[rows : rows + 1, :rows]
    other = halves(far_ref[:rows, :])
    out_ref[...] = in_ref[...] + pull((high_ref[...], low_ref[...]), other, own_tags, tags, heat, bias)


def far_picture_kernel(
    heat_ref, bias_ref, own_ref, scale_ref, high_ref, low_ref, far_ref, in_ref, out_ref
):
    heat, bias = scalars(heat_ref, bias_ref)
    rows = out_ref.shape[0]
    own_tags = column_of(own_ref[rows : rows + 1, :rows])
    tags = far_ref[rows : rows + 1, :rows]
    other = halves(far_ref[:rows, :])
    total = in_ref[...] + pull((high_ref[...], low_ref[...]), other, own_tags, tags, heat, bias)
    out_ref[...] = through_norm(total, own_ref[:rows, :], scale_ref[:, :1], heat)


def near_kernel(
    heat_ref, bias_ref, picture_ref, scale_ref,
    picture_high_ref, picture_low_ref, caption_high_ref, caption_low_ref,
    near_caption_ref, near_picture_ref, p_in_ref, c_in_ref, *refs,
):
    parts, (p_ref, c_ref, block) = refs[:PARTS], refs[PARTS:]
    heat, bias = scalars(heat_ref, bias_ref)
    rows = p_ref.shape[0]
    own_tags = column_of(picture_ref[rows : rows + 1, :rows])
    place = lax.rem(lax.axis_index("dp"), PLANE)

    def whole(near_ref, relayed):
        @pl.when(relayed)
        def _():
            step = rows // PARTS
            for k, part in enumerate(parts):
                block[k * step : (k + 1) * step, :] = part[:step, :]
            block[rows:, :] = parts[0][step:, :]

        @pl.when(jnp.logical_not(relayed))
        def _():
            block[...] = near_ref[...]

        return halves(block[:rows, :]), block[rows : rows + 1, :rows]

    other, tags = whole(near_caption_ref, place == 0)
    own = picture_high_ref[...], picture_low_ref[...]
    total = p_in_ref[...] + pull(own, other, own_tags, tags, heat, bias)
    p_ref[...] = through_norm(total, picture_ref[:rows, :], scale_ref[:, :1], heat)
    other, tags = whole(near_picture_ref, place == PLANE - 1)
    own = caption_high_ref[...], caption_low_ref[...]
    c_ref[...] = c_in_ref[...] + pull(own, other, own_tags, tags, heat, bias)


def call(kernel, out_shape, *operands, in_hbm=0, scratch=()):
    specs = [pl.BlockSpec(memory_space=pl.ANY)] * in_hbm
    specs += [SMEM if x.size == 1 else VMEM for x in operands[in_hbm:]]
    return pl.pallas_call(
        kernel,
        out_shape=out_shape,
        in_specs=specs,
        out_specs=[VMEM] * len(out_shape),
        scratch_shapes=scratch,
        compiler_params=pltpu.CompilerParams(vmem_limit_bytes=24 * 1024 * 1024),
        cost_estimate=pl.CostEstimate(flops=1024, bytes_accessed=1024, transcendentals=0),
    )(*operands)


def local(picture, caption, tags, heat, bias):
    half = lax.axis_size("dp") // 2
    rows, width = picture.shape
    step = rows // PARTS

    def f32(n, m=width):
        return jax.ShapeDtypeStruct((n, m), jnp.float32)

    def b16(n):
        return jax.ShapeDtypeStruct((n, width), jnp.bfloat16)

    caption, picture, caption_scale, picture_scale, *parts = call(
        unit_kernel,
        [f32(rows + 8)] * 2 + [f32(rows, 128)] * 2 + [f32(step + 8)] + [f32(step)] * (PARTS - 1),
        caption, picture, tags[None, :],
        in_hbm=2,
        scratch=[pltpu.VMEM((2, rows, width), jnp.float32), pltpu.SemaphoreType.DMA((2,))],
    )
    far_caption = shift(caption, half)
    far_picture = shift(picture, half)
    parts = [outward(part, to) for part, to in zip(parts, (None, *RELAYS), strict=True)]
    parts[1:] = [homeward(part, by) for part, by in zip(parts[1:], RELAYS, strict=True)]
    near_caption = shift(caption, 1, skip=True)
    near_picture = shift(picture, -1, skip=True)
    *units, p, c = call(
        own_kernel, [b16(rows)] * 4 + [f32(rows)] * 2, heat, bias, caption, picture
    )
    (p,) = call(
        far_caption_kernel, [f32(rows)], heat, bias, picture, *units[:2], far_caption, p
    )
    p, c = call(
        near_kernel, [f32(rows)] * 2,
        heat, bias, picture, picture_scale, *units, near_caption, near_picture, p, c, *parts,
        scratch=[pltpu.VMEM((rows + 8, width), jnp.float32)],
    )
    (c,) = call(
        far_picture_kernel, [f32(rows)],
        heat, bias, caption, caption_scale, *units[2:], far_picture, c,
    )
    return p, c


def solution(mesh):
    return jax.shard_map(
        local,
        mesh=mesh,
        in_specs=(P("dp", None), P("dp", None), P("dp"), P(), P()),
        out_specs=(P("dp", None), P("dp", None)),
        check_vma=False,
    )
```

time: 87.5 us -> 71.9 us (0.82)
  the two profiles are of different devices: /device:TPU:494 before, /device:TPU:16 now
where the time goes in v1:
time: 71.9 us; the launch traced here: 71.5 us
  starting transfers between devices  31.4 us (44%)
  Pallas kernels  18.8 us (26%)
  waiting for transfers between devices  16 us (22%)
  local copies, waits for them, and re-layouts  3.22 us (4%)
  between operations  2.05 us (3%)
    pallas_call x5, Pallas kernels, call(): pl.pallas_call(kernel, out_shape=out_shape, in_specs=specs, out_specs=[VM...  18.8 us
    ppermute x4, starting transfers between devices, shift(): return lax.ppermute(block, 'dp', route)  15.8 us
    ppermute x3, starting transfers between devices, outward(): return lax.ppermute(block, 'dp', route)  13.1 us
    ppermute x3, waiting for transfers between devices, outward(): return lax.ppermute(block, 'dp', route)  9.72 us
    ppermute x4, waiting for transfers between devices, shift(): return lax.ppermute(block, 'dp', route)  4.92 us
    ppermute x2, starting transfers between devices, homeward(): return lax.ppermute(block, 'dp', route)  2.56 us
    unnamed x4, local copies, waits for them, and re-layouts  2.54 us
  transfers between devices with their start and end apart: 9, of which 4 were waited for; matrix products, arithmetic and copies ran while one was open for 0% of the time, Pallas kernels for 19%

profile of v1, /device:TPU:16, one launch (start us, length us, event | category | flops | bytes accessed | tf_op | source)
XLA Modules:
  0.0 71.5 jit_solution(9285781755900747068)
XLA Ops:
  0.6 0.7 broadcast_in_dim.3.tags_ref
  1.3 1.3 %copy-done = f32[384,768]{1,0:T(8,128)S(1)} copy-done((f32[384,768]{1,0:T(8,128)S(1)}, f32[384,768]{1,0:T(8,128)}, u32[]{:S(2)}) %copy-start) | copy-done | bytes 1179672
  2.6 1.3 %copy-done.1 = f32[384,768]{1,0:T(8,128)S(1)} copy-done((f32[384,768]{1,0:T(8,128)S(1)}, f32[384,768]{1,0:T(8,128)}, u32[]{:S(2)}) %copy-start.1) | copy-done | bytes 1179672
  3.9 0.9 %shard_map.68 = (f32[392,768]{1,0:T(8,128)S(1)}, f32[392,768]{1,0:T(8,128)S(1)}, f32[384,128]{1,0:T(8,128)S(1)}, f32[384,128]{1,0:T(8,128)S(1)}, f32[136,768]{1,...) custom-call(f32[384,768]{1,0:T(8,128)S(1)} %copy-done, f32[384,768]{1,0:T(8,128)S(1)} %copy-done.1, ...), custom_call_target="tpu_custom_call" | custom-call | flops 1024 | bytes 1024 | tf_op jit(solution)/shard_map/pallas_call | solution.py:207
  4.8 7.6 %collective-permute-start.2 = (f32[392,768]{1,0:T(8,128)S(1)}, f32[392,768]{1,0:T(8,128)S(1)}, u32[]{:S(2)}, u32[]{:S(2)}) collective-permute-start(f32[392,768]{1,0:T(8,128)S(1)} %get-tuple-element.19.caption_ref.own_ref), channel_id=1, source_target_pairs={{0,256},{1,257},{2,258},{3,259},{4,260},{5,261},{6,262},{7,263},{8... | collective-permute-start | bytes 3612680 | tf_op jit(solution)/shard_map/ppermute | solution.py:25
  12.4 7.0 %collective-permute-start.4 = (f32[128,768]{1,0:T(8,128)S(1)}, f32[128,768]{1,0:T(8,128)S(1)}, u32[]{:S(2)}, u32[]{:S(2)}) collective-permute-start(f32[128,768]{1,0:T(8,128)S(1)} %get-tuple-element.27), channel_id=1, source_target_pairs={{127,158},{0,415},{255,286},{128,31},{383,414},{256,159},{511,30},... | collective-permute-start | bytes 1179656 | tf_op jit(solution)/shard_map/ppermute | solution.py:40
  19.4 1.3 %collective-permute-start.6 = (f32[128,768]{1,0:T(8,128)S(1)}, f32[128,768]{1,0:T(8,128)S(1)}, u32[]{:S(2)}, u32[]{:S(2)}) collective-permute-start(f32[128,768]{1,0:T(8,128)S(1)} %get-tuple-element.28), channel_id=1, source_target_pairs={{127,224},{0,481},{255,352},{128,97},{383,480},{256,225},{511,96},... | collective-permute-start | bytes 1179656 | tf_op jit(solution)/shard_map/ppermute | solution.py:40
  20.7 1.3 %collective-permute-start.1 = (f32[392,768]{1,0:T(8,128)S(1)}, f32[392,768]{1,0:T(8,128)S(1)}, u32[]{:S(2)}, u32[]{:S(2)}) collective-permute-start(f32[392,768]{1,0:T(8,128)S(1)} %get-tuple-element.17.picture_ref.own_ref), channel_id=1, source_target_pairs={{1,0},{2,1},{3,2},{4,3},{5,4},{6,5},{7,6},{8,7},{9,8},{10,9},{11,1... | collective-permute-start | bytes 3612680 | tf_op jit(solution)/shard_map/ppermute | solution.py:25
  22.0 3.1 %collective-permute-start = (f32[392,768]{1,0:T(8,128)S(1)}, f32[392,768]{1,0:T(8,128)S(1)}, u32[]{:S(2)}, u32[]{:S(2)}) collective-permute-start(f32[392,768]{1,0:T(8,128)S(1)} %get-tuple-element.19.caption_ref.own_ref), channel_id=1, source_target_pairs={{0,1},{1,2},{2,3},{3,4},{4,5},{5,6},{6,7},{7,8},{8,9},{9,10},{10,1... | collective-permute-start | bytes 3612680 | tf_op jit(solution)/shard_map/ppermute | solution.py:25
  25.1 0.0 collective-permute-done.4
  25.2 3.7 %collective-permute-start.8 = (f32[392,768]{1,0:T(8,128)S(1)}, f32[392,768]{1,0:T(8,128)S(1)}, u32[]{:S(2)}, u32[]{:S(2)}) collective-permute-start(f32[392,768]{1,0:T(8,128)S(1)} %get-tuple-element.17.picture_ref.own_ref), channel_id=1, source_target_pairs={{0,256},{1,257},{2,258},{3,259},{4,260},{5,261},{6,262},{7,263},{8... | collective-permute-start | bytes 3612680 | tf_op jit(solution)/shard_map/ppermute | solution.py:25
  28.9 0.0 collective-permute-done.6
  28.9 4.8 %collective-permute-start.3 = (f32[136,768]{1,0:T(8,128)S(1)}, f32[136,768]{1,0:T(8,128)S(1)}, u32[]{:S(2)}, u32[]{:S(2)}) collective-permute-start(f32[136,768]{1,0:T(8,128)S(1)} %get-tuple-element.26), channel_id=1, source_target_pairs={{127,128},{0,511},{255,256},{128,127},{383,384},{256,255},{511,0},... | collective-permute-start | bytes 1253384 | tf_op jit(solution)/shard_map/ppermute | solution.py:40
  33.7 9.7 %collective-permute-done.3.refs_0_ = f32[136,768]{1,0:T(8,128)S(1)} collective-permute-done((f32[136,768]{1,0:T(8,128)S(1)}, f32[136,768]{1,0:T(8,128)S(1)}, u32[]{:S(2)}, u32[]{:S(2)}) %collective-permute-start.3) | collective-permute-done | bytes 417824 | tf_op jit(solution)/shard_map/ppermute | solution.py:40
  43.4 1.3 %collective-permute-start.5 = (f32[128,768]{1,0:T(8,128)S(1)}, f32[128,768]{1,0:T(8,128)S(1)}, u32[]{:S(2)}, u32[]{:S(2)}) collective-permute-start(f32[128,768]{1,0:T(8,128)S(1)} %collective-permute-done.4), channel_id=1, source_target_pairs={{30,0},{31,127},{158,128},{159,255},{286,256},{287,383},{414,384},... | collective-permute-start | bytes 1179656 | tf_op jit(solution)/shard_map/ppermute | solution.py:49
  44.7 0.5 collective-permute-done.2.far_ref
  45.2 1.3 %collective-permute-start.7 = (f32[128,768]{1,0:T(8,128)S(1)}, f32[128,768]{1,0:T(8,128)S(1)}, u32[]{:S(2)}, u32[]{:S(2)}) collective-permute-start(f32[128,768]{1,0:T(8,128)S(1)} %collective-permute-done.6), channel_id=1, source_target_pairs={{96,0},{97,127},{224,128},{225,255},{352,256},{353,383},{480,384},... | collective-permute-start | bytes 1179656 | tf_op jit(solution)/shard_map/ppermute | solution.py:49
  47.8 4.2 %shard_map.69 = (bf16[384,768]{1,0:T(8,128)(2,1)S(1)}, bf16[384,768]{1,0:T(8,128)(2,1)S(1)}, bf16[384,768]{1,0:T(8,128)(2,1)S(1)}, bf16[384,768]{1,0:T(8,128)(2,...) custom-call(f32[1]{0:T(128)S(6)} %copy.7.heat_ref, f32[1]{0:T(128)S(6)} %copy.8.bias_ref, ...), custom_call_target="tpu_custom_call" | custom-call | flops 1024 | bytes 1024 | tf_op jit(solution)/shard_map/pallas_call | solution.py:207
  52.0 2.7 %shard_map.70.p_in_ref = f32[384,768]{1,0:T(8,128)S(1)} custom-call(f32[1]{0:T(128)S(6)} %copy.7.heat_ref, f32[1]{0:T(128)S(6)} %copy.8.bias_ref, f32[392,768]{1,0:T(8,128)S(1)} %get-tuple-element.17.picture_ref.own_ref, bf16[384,768]{1,0:T(8,128)(2,1)S(1)} %get-tuple-element.20.high_ref.picture_high_ref, ...), custom_call_target="tpu_custom_call" | custom-call | flops 1024 | bytes 1024 | tf_op jit(solution)/shard_map/pallas_call | solution.py:207
  54.7 0.0 collective-permute-done.5.refs_1_
  54.7 1.4 %collective-permute-done.7.refs_2_ = f32[128,768]{1,0:T(8,128)S(1)} collective-permute-done((f32[128,768]{1,0:T(8,128)S(1)}, f32[128,768]{1,0:T(8,128)S(1)}, u32[]{:S(2)}, u32[]{:S(2)}) %collective-permute-start.7) | collective-permute-done | bytes 393248 | tf_op jit(solution)/shard_map/ppermute | solution.py:49
  56.1 7.1 %shard_map.71 = (f32[384,768]{1,0:T(8,128)}, f32[384,768]{1,0:T(8,128)S(1)}) custom-call(f32[1]{0:T(128)S(6)} %copy.7.heat_ref, f32[1]{0:T(128)S(6)} %copy.8.bias_ref, f32[392,768]{1,0:T(8,128)S(1)} %get-tuple-element.17.picture_ref.own_ref, f32[384,128]{1,0:T(8,128)S(1)} %get-tuple-element.18.scale_ref, ...), custom_call_target="tpu_custom_call" | custom-call | flops 1024 | bytes 1024 | tf_op jit(solution)/shard_map/pallas_call | solution.py:207
  63.2 4.4 %collective-permute-done.8.far_ref = f32[392,768]{1,0:T(8,128)S(1)} collective-permute-done((f32[392,768]{1,0:T(8,128)S(1)}, f32[392,768]{1,0:T(8,128)S(1)}, u32[]{:S(2)}, u32[]{:S(2)}) %collective-permute-start.8) | collective-permute-done | bytes 1204256 | tf_op jit(solution)/shard_map/ppermute | solution.py:25
  67.6 3.9 %shard_map.72 = f32[384,768]{1,0:T(8,128)} custom-call(f32[1]{0:T(128)S(6)} %copy.7.heat_ref, f32[1]{0:T(128)S(6)} %copy.8.bias_ref, f32[392,768]{1,0:T(8,128)S(1)} %get-tuple-element.19.caption_ref.own_ref, f32[384,128]{1,0:T(8,128)S(1)} %get-tuple-element.30.scale_ref, bf16[384,768]{1,0:T(8,128)(2,1)S(1)} %get-tuple-element.22.caption_high_ref.high_ref, ...), custom_call_target="tpu_custom_call" | custom-call | flops 1024 | bytes 1024 | tf_op jit(solution)/shard_map/pallas_call | solution.py:207
  (4 shorter events, 0.0 us)
Async XLA Ops:
  1.3 1.3 %copy-start = (f32[384,768]{1,0:T(8,128)S(1)}, f32[384,768]{1,0:T(8,128)}, u32[]{:S(2)}) copy-start(f32[384,768]{1,0:T(8,128)} %caption_ref.1) | copy-start | bytes 3538948
  2.6 1.3 %copy-start.1 = (f32[384,768]{1,0:T(8,128)S(1)}, f32[384,768]{1,0:T(8,128)}, u32[]{:S(2)}) copy-start(f32[384,768]{1,0:T(8,128)} %picture_ref.1) | copy-start | bytes 3538948
  4.8 40.4 %collective-permute-start.2 = (f32[392,768]{1,0:T(8,128)S(1)}, f32[392,768]{1,0:T(8,128)S(1)}, u32[]{:S(2)}, u32[]{:S(2)}) collective-permute-start(f32[392,768]{1,0:T(8,128)S(1)} %get-tuple-element.19.caption_ref.own_ref), channel_id=1, source_target_pairs={{0,256},{1,257},{2,258},{3,259},{4,260},{5,261},{6,262},{7,263},{8... | collective-permute-start | bytes 3612680 | tf_op jit(solution)/shard_map/ppermute | solution.py:25
  12.4 12.7 %collective-permute-start.4 = (f32[128,768]{1,0:T(8,128)S(1)}, f32[128,768]{1,0:T(8,128)S(1)}, u32[]{:S(2)}, u32[]{:S(2)}) collective-permute-start(f32[128,768]{1,0:T(8,128)S(1)} %get-tuple-element.27), channel_id=1, source_target_pairs={{127,158},{0,415},{255,286},{128,31},{383,414},{256,159},{511,30},... | collective-permute-start | bytes 1179656 | tf_op jit(solution)/shard_map/ppermute | solution.py:40
  19.4 9.5 %collective-permute-start.6 = (f32[128,768]{1,0:T(8,128)S(1)}, f32[128,768]{1,0:T(8,128)S(1)}, u32[]{:S(2)}, u32[]{:S(2)}) collective-permute-start(f32[128,768]{1,0:T(8,128)S(1)} %get-tuple-element.28), channel_id=1, source_target_pairs={{127,224},{0,481},{255,352},{128,97},{383,480},{256,225},{511,96},... | collective-permute-start | bytes 1179656 | tf_op jit(solution)/shard_map/ppermute | solution.py:40
  20.7 35.4 %collective-permute-start.1 = (f32[392,768]{1,0:T(8,128)S(1)}, f32[392,768]{1,0:T(8,128)S(1)}, u32[]{:S(2)}, u32[]{:S(2)}) collective-permute-start(f32[392,768]{1,0:T(8,128)S(1)} %get-tuple-element.17.picture_ref.own_ref), channel_id=1, source_target_pairs={{1,0},{2,1},{3,2},{4,3},{5,4},{6,5},{7,6},{8,7},{9,8},{10,9},{11,1... | collective-permute-start | bytes 3612680 | tf_op jit(solution)/shard_map/ppermute | solution.py:25
  22.0 34.1 %collective-permute-start = (f32[392,768]{1,0:T(8,128)S(1)}, f32[392,768]{1,0:T(8,128)S(1)}, u32[]{:S(2)}, u32[]{:S(2)}) collective-permute-start(f32[392,768]{1,0:T(8,128)S(1)} %get-tuple-element.19.caption_ref.own_ref), channel_id=1, source_target_pairs={{0,1},{1,2},{2,3},{3,4},{4,5},{5,6},{6,7},{7,8},{8,9},{9,10},{10,1... | collective-permute-start | bytes 3612680 | tf_op jit(solution)/shard_map/ppermute | solution.py:25
  25.2 42.4 %collective-permute-start.8 = (f32[392,768]{1,0:T(8,128)S(1)}, f32[392,768]{1,0:T(8,128)S(1)}, u32[]{:S(2)}, u32[]{:S(2)}) collective-permute-start(f32[392,768]{1,0:T(8,128)S(1)} %get-tuple-element.17.picture_ref.own_ref), channel_id=1, source_target_pairs={{0,256},{1,257},{2,258},{3,259},{4,260},{5,261},{6,262},{7,263},{8... | collective-permute-start | bytes 3612680 | tf_op jit(solution)/shard_map/ppermute | solution.py:25
  28.9 14.5 %collective-permute-start.3 = (f32[136,768]{1,0:T(8,128)S(1)}, f32[136,768]{1,0:T(8,128)S(1)}, u32[]{:S(2)}, u32[]{:S(2)}) collective-permute-start(f32[136,768]{1,0:T(8,128)S(1)} %get-tuple-element.26), channel_id=1, source_target_pairs={{127,128},{0,511},{255,256},{128,127},{383,384},{256,255},{511,0},... | collective-permute-start | bytes 1253384 | tf_op jit(solution)/shard_map/ppermute | solution.py:40
  43.4 11.3 %collective-permute-start.5 = (f32[128,768]{1,0:T(8,128)S(1)}, f32[128,768]{1,0:T(8,128)S(1)}, u32[]{:S(2)}, u32[]{:S(2)}) collective-permute-start(f32[128,768]{1,0:T(8,128)S(1)} %collective-permute-done.4), channel_id=1, source_target_pairs={{30,0},{31,127},{158,128},{159,255},{286,256},{287,383},{414,384},... | collective-permute-start | bytes 1179656 | tf_op jit(solution)/shard_map/ppermute | solution.py:49
  45.2 10.9 %collective-permute-start.7 = (f32[128,768]{1,0:T(8,128)S(1)}, f32[128,768]{1,0:T(8,128)S(1)}, u32[]{:S(2)}, u32[]{:S(2)}) collective-permute-start(f32[128,768]{1,0:T(8,128)S(1)} %collective-permute-done.6), channel_id=1, source_target_pairs={{96,0},{97,127},{224,128},{225,255},{352,256},{353,383},{480,384},... | collective-permute-start | bytes 1179656 | tf_op jit(solution)/shard_map/ppermute | solution.py:49

commit v2 on v1

v2 whole, which is shorter than its diff:
```python
import jax
import jax.numpy as jnp
from jax import lax
from jax.experimental import pallas as pl
from jax.experimental.pallas import tpu as pltpu
from jax.sharding import PartitionSpec as P

NT = (((1,), (1,)), ((), ()))
NN = (((1,), (0,)), ((), ()))
PLANE = 128
DEEP = 16
UP_BY = ((0, 15), (3, 0), (2, 15), (3, 14))
DOWN_BY = ((0, 15), (3, 0), (1, 0), (0, 1))
PARTS = len(UP_BY)
FAR_COST = 1 << 37
VMEM = pl.BlockSpec(memory_space=pltpu.VMEM)
SMEM = pl.BlockSpec(memory_space=pltpu.SMEM)


def swap(block, to):
    count = lax.axis_size("dp")
    route = [(i, to(i) % count) for i in range(count)]
    return lax.ppermute(block, "dp", [pair for pair in route if pair[0] != pair[1]])


def over_core(i):
    return i ^ 1


def over_chip(i):
    j = i + 1 if i % 2 else i - 1
    return j if i // PLANE == j // PLANE else i


def relays(k):
    up, down = UP_BY[k], DOWN_BY[k]
    return (up[0] * DEEP + up[1]) * 2, (down[0] * DEEP + down[1]) * 2 + 1


def outward(block, k):
    count = lax.axis_size("dp")
    up, down = relays(k)
    route = []
    for plane in range(0, count, PLANE):
        route.append((plane + PLANE - 1, (plane + PLANE) % count + up))
        route.append((plane, (plane - PLANE) % count + down))
    return lax.ppermute(block, "dp", route)


def homeward(block, k):
    count = lax.axis_size("dp")
    up, down = relays(k)
    route = []
    for plane in range(0, count, PLANE):
        route.append((plane + up, plane))
        route.append((plane + down, plane + PLANE - 1))
    return lax.ppermute(block, "dp", route)


def inverse_norm(rows):
    return lax.rsqrt(jnp.sum(rows * rows, axis=-1, keepdims=True) + 1e-06)


def halves(value):
    high = value.astype(jnp.bfloat16)
    low = (value - high.astype(jnp.float32)).astype(jnp.bfloat16)
    return high, low


def dot(left, right, dims):
    return lax.dot_general(left, right, dims, preferred_element_type=jnp.float32)


def dot_nt(left, right):
    count = right[0].shape[0]
    both = dot(left[0], jnp.concatenate(right, axis=0), NT)
    return both[:, :count] + (both[:, count:] + dot(left[1], right[0], NT))


def dot_nn(left, right):
    high, low = right
    left = jnp.concatenate([left[0], left[0], left[1]], axis=1)
    return dot(left, jnp.concatenate([high, low, high], axis=0), NN)


def column_of(row):
    return jnp.transpose(jnp.broadcast_to(row, (8, row.shape[1])))[:, :1]


def slopes(own, other, own_tags, other_tags, heat, bias):
    logit = heat * dot_nt(own, other) + bias
    return 1.0 / (1.0 + jnp.exp(-logit)) - jnp.where(own_tags == other_tags, 1.0, 0.0)


def pull(own, other, *tags_and_scalars):
    return dot_nn(halves(slopes(own, other, *tags_and_scalars)), other)


def scalars(heat_ref, bias_ref):
    return jnp.exp(jnp.full((1, 1), heat_ref[0], jnp.float32)), bias_ref[0]


def through_norm(total, unit, scale, heat):
    total = heat * total
    return scale * (total - unit * jnp.sum(unit * total, axis=-1, keepdims=True))


def put_tags(ref, tags):
    count = ref.shape[0] - 8
    ref[count:, :] = jnp.zeros((8, ref.shape[1]), jnp.float32)
    ref[count : count + 1, : tags.shape[1]] = tags


def is_even():
    return lax.rem(lax.axis_index("dp"), 2) == 0


def stage_kernel(caption_ref, tags_ref, out_ref):
    out_ref[: caption_ref.shape[0], :] = caption_ref[...]
    put_tags(out_ref, tags_ref[...].astype(jnp.float32))


def unit_kernel(
    staged_ref, picture_ref,
    caption_out, picture_out, core_out, chip_out, own_tags_out, caption_scale, picture_scale, *parts,
):
    rows = picture_ref.shape[0]
    even = is_even()
    tags = staged_ref[rows : rows + 1, :rows]
    own_tags_out[...] = jnp.broadcast_to(column_of(tags), own_tags_out.shape)
    units = []
    for source, out, scale_out in (
        (staged_ref, caption_out, caption_scale),
        (picture_ref, picture_out, picture_scale),
    ):
        value = source[:rows, :]
        scale = inverse_norm(value)
        units.append(value * scale)
        out[...] = units[-1]
        scale_out[...] = jnp.broadcast_to(scale, scale_out.shape)
    caption, picture = units
    core_out[:rows, :] = jnp.where(even, caption, picture)
    put_tags(core_out, tags)
    chip = jnp.where(even, picture, caption)
    chip_out[:rows, :] = chip
    put_tags(chip_out, tags)
    step = rows // PARTS
    for k, part in enumerate(parts):
        part[:step, :] = chip[k * step : (k + 1) * step, :]
    put_tags(parts[0], tags)


def place_in_plane():
    return lax.rem(lax.axis_index("dp"), PLANE)


def own_kernel(
    heat_ref, bias_ref, own_tags_ref, staged_ref, caption_ref, picture_ref,
    caption_high_ref, caption_low_ref, picture_high_ref, picture_low_ref, c_ref, p_ref,
):
    heat, bias = scalars(heat_ref, bias_ref)
    rows = c_ref.shape[0]
    tags = staged_ref[rows : rows + 1, :rows]
    caption, picture = halves(caption_ref[...]), halves(picture_ref[...])
    caption_high_ref[...], caption_low_ref[...] = caption
    picture_high_ref[...], picture_low_ref[...] = picture
    slope = slopes(caption, picture, own_tags_ref[:, :1], tags, heat, bias)
    c_ref[...] = dot_nn(halves(slope), picture)
    p_ref[...] = dot_nn(halves(jnp.transpose(slope)), caption)


def far_kernel(heat_ref, bias_ref, own_tags_ref, high_ref, low_ref, far_ref, in_ref, out_ref):
    heat, bias = scalars(heat_ref, bias_ref)
    rows = out_ref.shape[0]
    other = far_ref[:rows, :]
    own, other = (high_ref[...], low_ref[...]), halves(other * inverse_norm(other))
    tags = far_ref[rows : rows + 1, :rows]
    out_ref[...] = in_ref[...] + pull(own, other, own_tags_ref[:, :1], tags, heat, bias)


def near_pull(heat, bias, own_tags_ref, caption, picture, of_caption, other_ref):
    rows = other_ref.shape[0] - 8
    own = [jnp.where(of_caption, c[...], p[...]) for c, p in zip(caption, picture, strict=True)]
    tags = other_ref[rows : rows + 1, :rows]
    return pull(own, halves(other_ref[:rows, :]), own_tags_ref[:, :1], tags, heat, bias)


def core_kernel(
    heat_ref, bias_ref, own_tags_ref,
    caption_high_ref, caption_low_ref, picture_high_ref, picture_low_ref,
    other_ref, c_in_ref, p_in_ref, c_ref, p_ref,
):
    heat, bias = scalars(heat_ref, bias_ref)
    even = is_even()
    caption, picture = (caption_high_ref, caption_low_ref), (picture_high_ref, picture_low_ref)
    more = near_pull(heat, bias, own_tags_ref, caption, picture, even, other_ref)
    c_ref[...] = c_in_ref[...] + jnp.where(even, more, 0.0)
    p_ref[...] = p_in_ref[...] + jnp.where(even, 0.0, more)


def chip_kernel(
    heat_ref, bias_ref, own_tags_ref, picture_ref, scale_ref,
    caption_high_ref, caption_low_ref, picture_high_ref, picture_low_ref,
    other_ref, c_in_ref, p_in_ref, *refs,
):
    parts, (c_ref, p_ref, block) = refs[:PARTS], refs[PARTS:]
    heat, bias = scalars(heat_ref, bias_ref)
    rows = c_ref.shape[0]
    step = rows // PARTS
    even = is_even()
    place = place_in_plane()
    in_parts = jnp.logical_or(place == 0, place == PLANE - 1)

    @pl.when(in_parts)
    def _():
        for k, part in enumerate(parts):
            block[k * step : (k + 1) * step, :] = part[:step, :]
        block[rows:, :] = parts[0][step:, :]

    @pl.when(jnp.logical_not(in_parts))
    def _():
        block[...] = other_ref[...]

    caption, picture = (caption_high_ref, caption_low_ref), (picture_high_ref, picture_low_ref)
    more = near_pull(heat, bias, own_tags_ref, caption, picture, jnp.logical_not(even), block)
    c_ref[...] = c_in_ref[...] + jnp.where(even, 0.0, more)
    total = p_in_ref[...] + jnp.where(even, more, 0.0)
    p_ref[...] = through_norm(total, picture_ref[...], scale_ref[:, :1], heat)


def last_kernel(
    heat_ref, bias_ref, own_tags_ref, unit_ref, scale_ref, high_ref, low_ref, far_ref, tags_ref,
    in_ref, out_ref,
):
    heat, bias = scalars(heat_ref, bias_ref)
    rows = out_ref.shape[0]
    own, other = (high_ref[...], low_ref[...]), halves(far_ref[...])
    tags = tags_ref[rows : rows + 1, :rows]
    total = in_ref[...] + pull(own, other, own_tags_ref[:, :1], tags, heat, bias)
    out_ref[...] = through_norm(total, unit_ref[...], scale_ref[:, :1], heat)


def call(kernel, out_shape, *operands, cost=1024, scratch=()):
    return pl.pallas_call(
        kernel,
        out_shape=out_shape,
        in_specs=[SMEM if x.size == 1 else VMEM for x in operands],
        out_specs=[VMEM] * len(out_shape),
        scratch_shapes=scratch,
        compiler_params=pltpu.CompilerParams(vmem_limit_bytes=24 * 1024 * 1024),
        cost_estimate=pl.CostEstimate(flops=cost, bytes_accessed=1024, transcendentals=0),
    )(*operands)


def local(picture, caption, tags, heat, bias):
    count = lax.axis_size("dp")
    rows, width = picture.shape
    step = rows // PARTS

    def f32(n, m=width):
        return jax.ShapeDtypeStruct((n, m), jnp.float32)

    def b16(n):
        return jax.ShapeDtypeStruct((n, width), jnp.bfloat16)

    def over_half(i):
        return i + count // 2

    (staged,) = call(stage_kernel, [f32(rows + 8)], caption, tags[None, :])
    far_caption = swap(staged, over_half)
    caption, picture, core, chip, own_tags, caption_scale, picture_scale, *parts = call(
        unit_kernel,
        [f32(rows)] * 2 + [f32(rows + 8)] * 2 + [f32(rows, 128)] * 3
        + [f32(step + 8)] + [f32(step)] * (PARTS - 1),
        staged, picture,
    )
    parts = [outward(part, k) for k, part in enumerate(parts)]
    parts = [homeward(part, k) for k, part in enumerate(parts)]
    core = swap(core, over_core)
    chip = swap(chip, over_chip)
    far_picture = swap(picture, over_half)
    scalar = heat, bias, own_tags
    *units, c, p = call(
        own_kernel, [b16(rows)] * 4 + [f32(rows)] * 2, *scalar, staged, caption, picture
    )
    (p,) = call(far_kernel, [f32(rows)], *scalar, *units[2:], far_caption, p, cost=FAR_COST)
    c, p = call(core_kernel, [f32(rows)] * 2, *scalar, *units, core, c, p)
    c, p = call(
        chip_kernel, [f32(rows)] * 2,
        *scalar, picture, picture_scale, *units, chip, c, p, *parts,
        scratch=[pltpu.VMEM((rows + 8, width), jnp.float32)],
    )
    (c,) = call(
        last_kernel, [f32(rows)],
        *scalar, caption, caption_scale, *units[:2], far_picture, far_caption, c,
    )
    return p, c


def solution(mesh):
    return jax.shard_map(
        local,
        mesh=mesh,
        in_specs=(P("dp", None), P("dp", None), P("dp"), P(), P()),
        out_specs=(P("dp", None), P("dp", None)),
        check_vma=False,
    )
```

time: 71.9 us -> 68.5 us (0.953)
  the two profiles are of different devices: /device:TPU:16 before, /device:TPU:22 now
where the time goes in v2:
time: 68.5 us; the launch traced here: 68 us
  waiting for transfers between devices  30.8 us (45%)
  starting transfers between devices  18.3 us (27%)
  Pallas kernels  14.9 us (22%)
  between operations  2.14 us (3%)
  local copies, waits for them, and re-layouts  1.96 us (3%)
    ppermute x4, waiting for transfers between devices, outward(): return lax.ppermute(block, 'dp', route)  16.9 us
    pallas_call x7, Pallas kernels, call(): pl.pallas_call(kernel, out_shape=out_shape, in_specs=[SMEM if x.size == 1...  14.9 us
    ppermute x4, waiting for transfers between devices, swap(): lax.ppermute(block, 'dp', [pair for pair in route if pair[0] != pair[1]])  13.9 us
    ppermute x4, starting transfers between devices, swap(): lax.ppermute(block, 'dp', [pair for pair in route if pair[0] != pair[1]])  11.6 us
    ppermute x4, starting transfers between devices, homeward(): return lax.ppermute(block, 'dp', route)  3.34 us
    ppermute x4, starting transfers between devices, outward(): return lax.ppermute(block, 'dp', route)  3.33 us
  transfers between devices with their start and end apart: 12, of which 2 were waited for; matrix products, arithmetic and copies ran while one was open for 0% of the time, Pallas kernels for 17%

profile of v2, /device:TPU:22, one launch (start us, length us, event | category | flops | bytes accessed | tf_op | source)
XLA Modules:
  0.0 68.0 jit_solution(7236335082287420344)
XLA Ops:
  0.6 0.7 %broadcast_in_dim.3.tags_ref = s32[1,384]{1,0:T(1,128)S(1)} reshape(s32[384]{0:T(512)} %param.7) | data formatting | bytes 3072 | tf_op jit(solution)/shard_map/broadcast_in_dim | solution.py:269
  1.3 1.3 %copy-done = f32[384,768]{1,0:T(8,128)S(1)} copy-done((f32[384,768]{1,0:T(8,128)S(1)}, f32[384,768]{1,0:T(8,128)}, u32[]{:S(2)}) %copy-start) | copy-done | bytes 1179672
  2.6 0.1 shard_map.68.staged_ref
  2.7 2.4 %collective-permute-start.2 = (f32[392,768]{1,0:T(8,128)S(1)}, f32[392,768]{1,0:T(8,128)S(1)}, u32[]{:S(2)}, u32[]{:S(2)}) collective-permute-start(f32[392,768]{1,0:T(8,128)S(1)} %shard_map.68.staged_ref), channel_id=1, source_target_pairs={{0,256},{1,257},{2,258},{3,259},{4,260},{5,261},{6,262},{7,263},{8... | collective-permute-start | bytes 3612680 | tf_op jit(solution)/shard_map/ppermute | solution.py:23
  5.1 0.7 %shard_map.69 = (f32[384,768]{1,0:T(8,128)S(1)}, f32[384,768]{1,0:T(8,128)S(1)}, f32[392,768]{1,0:T(8,128)S(1)}, f32[392,768]{1,0:T(8,128)S(1)}, f32[384,128]{1,...) custom-call(f32[392,768]{1,0:T(8,128)S(1)} %shard_map.68.staged_ref,, ...), custom_call_target="tpu_custom_call" | custom-call | flops 1024 | bytes 1024 | tf_op jit(solution)/shard_map/pallas_call | solution.py:244
  5.8 1.9 %collective-permute-start.1 = (f32[392,768]{1,0:T(8,128)S(1)}, f32[392,768]{1,0:T(8,128)S(1)}, u32[]{:S(2)}, u32[]{:S(2)}) collective-permute-start(f32[392,768]{1,0:T(8,128)S(1)} %get-tuple-element.32), channel_id=1, source_target_pairs={{0,1},{1,0},{2,3},{3,2},{4,5},{5,4},{6,7},{7,6},{8,9},{9,8},{10,11... | collective-permute-start | bytes 3612680 | tf_op jit(solution)/shard_map/ppermute | solution.py:23
  7.7 0.7 collective-permute-start.9
  8.4 1.3 %collective-permute-start.5 = (f32[96,768]{1,0:T(8,128)S(1)}, f32[96,768]{1,0:T(8,128)S(1)}, u32[]{:S(2)}, u32[]{:S(2)}) collective-permute-start(f32[96,768]{1,0:T(8,128)S(1)} %get-tuple-element.38), channel_id=1, source_target_pairs={{127,224},{0,481},{255,352},{128,97},{383,480},{256,225},{511,96},... | collective-permute-start | bytes 884744 | tf_op jit(solution)/shard_map/ppermute | solution.py:47
  9.7 0.7 %collective-permute-start.3 = (f32[104,768]{1,0:T(8,128)S(1)}, f32[104,768]{1,0:T(8,128)S(1)}, u32[]{:S(2)}, u32[]{:S(2)}) collective-permute-start(f32[104,768]{1,0:T(8,128)S(1)} %get-tuple-element.37), channel_id=1, source_target_pairs={{127,158},{0,415},{255,286},{128,31},{383,414},{256,159},{511,30},... | collective-permute-start | bytes 958472 | tf_op jit(solution)/shard_map/ppermute | solution.py:47
  10.4 0.0 collective-permute-done.9
  10.4 0.7 collective-permute-start.7
  11.1 16.9 %collective-permute-done.5 = f32[96,768]{1,0:T(8,128)S(1)} collective-permute-done((f32[96,768]{1,0:T(8,128)S(1)}, f32[96,768]{1,0:T(8,128)S(1)}, u32[]{:S(2)}, u32[]{:S(2)}) %collective-permute-start.5) | collective-permute-done | bytes 294944 | tf_op jit(solution)/shard_map/ppermute | solution.py:47
  28.0 0.7 collective-permute-start.10
  29.9 2.7 %shard_map.70 = (bf16[384,768]{1,0:T(8,128)(2,1)S(1)}, bf16[384,768]{1,0:T(8,128)(2,1)S(1)}, bf16[384,768]{1,0:T(8,128)(2,1)S(1)}, bf16[384,768]{1,0:T(8,128)(2,...) custom-call(f32[1]{0:T(128)S(6)} %copy.7.heat_ref, f32[1]{0:T(128)S(6)} %copy.8.bias_ref, ...), custom_call_target="tpu_custom_call" | custom-call | flops 1024 | bytes 1024 | tf_op jit(solution)/shard_map/pallas_call | solution.py:244
  32.6 5.4 %collective-permute-start.11 = (f32[384,768]{1,0:T(8,128)S(1)}, f32[384,768]{1,0:T(8,128)S(1)}, u32[]{:S(2)}, u32[]{:S(2)}) collective-permute-start(f32[384,768]{1,0:T(8,128)S(1)} %get-tuple-element.24.picture_ref), channel_id=1, source_target_pairs={{0,256},{1,257},{2,258},{3,259},{4,260},{5,261},{6,262},{7,263},{8... | collective-permute-start | bytes 3538952 | tf_op jit(solution)/shard_map/ppermute | solution.py:23
  38.0 1.9 %collective-permute-start = (f32[392,768]{1,0:T(8,128)S(1)}, f32[392,768]{1,0:T(8,128)S(1)}, u32[]{:S(2)}, u32[]{:S(2)}) collective-permute-start(f32[392,768]{1,0:T(8,128)S(1)} %get-tuple-element.31), channel_id=1, source_target_pairs={{1,2},{2,1},{3,4},{4,3},{5,6},{6,5},{7,8},{8,7},{9,10},{10,9},{11,... | collective-permute-start | bytes 3612680 | tf_op jit(solution)/shard_map/ppermute | solution.py:23
  40.0 1.3 %collective-permute-start.6 = (f32[96,768]{1,0:T(8,128)S(1)}, f32[96,768]{1,0:T(8,128)S(1)}, u32[]{:S(2)}, u32[]{:S(2)}) collective-permute-start(f32[96,768]{1,0:T(8,128)S(1)} %collective-permute-done.5), channel_id=1, source_target_pairs={{96,0},{97,127},{224,128},{225,255},{352,256},{353,383},{480,384},... | collective-permute-start | bytes 884744 | tf_op jit(solution)/shard_map/ppermute | solution.py:57
  41.3 0.7 collective-permute-start.8
  42.0 0.7 %collective-permute-start.4 = (f32[104,768]{1,0:T(8,128)S(1)}, f32[104,768]{1,0:T(8,128)S(1)}, u32[]{:S(2)}, u32[]{:S(2)}) collective-permute-start(f32[104,768]{1,0:T(8,128)S(1)} %collective-permute-done.3), channel_id=1, source_target_pairs={{30,0},{31,127},{158,128},{159,255},{286,256},{287,383},{414,384},... | collective-permute-start | bytes 958472 | tf_op jit(solution)/shard_map/ppermute | solution.py:57
  42.7 2.3 %shard_map.71.p_in_ref = f32[384,768]{1,0:T(8,128)S(1)} custom-call(f32[1]{0:T(128)S(6)} %copy.7.heat_ref, f32[1]{0:T(128)S(6)} %copy.8.bias_ref, f32[384,128]{1,0:T(8,128)S(1)} %get-tuple-element.23.own_tags_ref, bf16[384,768]{1,0:T(8,128)(2,1)S(1)} %get-tuple-element.29.high_ref.picture_high_ref, ...), custom_call_target="tpu_custom_call" | custom-call | flops 137438953472 | bytes 1024 | tf_op jit(solution)/shard_map/pallas_call | solution.py:244
  45.0 2.2 %shard_map.72 = (f32[384,768]{1,0:T(8,128)S(1)}, f32[384,768]{1,0:T(8,128)S(1)}) custom-call(f32[1]{0:T(128)S(6)} %copy.7.heat_ref, f32[1]{0:T(128)S(6)} %copy.8.bias_ref, f32[384,128]{1,0:T(8,128)S(1)} %get-tuple-element.23.own_tags_ref, bf16[384,768]{1,0:T(8,128)(2,1)S(1)} %get-tuple-element.27.caption_high_ref.high_ref, ...), custom_call_target="tpu_custom_call" | custom-call | flops 1024 | bytes 1024 | tf_op jit(solution)/shard_map/pallas_call | solution.py:244
  47.2 13.9 %collective-permute-done.other_ref = f32[392,768]{1,0:T(8,128)S(1)} collective-permute-done((f32[392,768]{1,0:T(8,128)S(1)}, f32[392,768]{1,0:T(8,128)S(1)}, u32[]{:S(2)}, u32[]{:S(2)}) %collective-permute-start) | collective-permute-done | bytes 1204256 | tf_op jit(solution)/shard_map/ppermute | solution.py:23
  61.1 3.5 %shard_map.73 = (f32[384,768]{1,0:T(8,128)S(1)}, f32[384,768]{1,0:T(8,128)}) custom-call(f32[1]{0:T(128)S(6)} %copy.7.heat_ref, f32[1]{0:T(128)S(6)} %copy.8.bias_ref, f32[384,128]{1,0:T(8,128)S(1)} %get-tuple-element.23.own_tags_ref, f32[384,768]{1,0:T(8,128)S(1)} %get-tuple-element.24.picture_ref, f32[384,128]{1,0:T(8,128)S(1)} %get-tuple-element.25.scale_ref, ...), custom_call_target="tpu_custom_call" | custom-call | flops 1024 | bytes 1024 | tf_op jit(solution)/shard_map/pallas_call | solution.py:244
  64.6 3.4 %shard_map.74 = f32[384,768]{1,0:T(8,128)} custom-call(f32[1]{0:T(128)S(6)} %copy.7.heat_ref, f32[1]{0:T(128)S(6)} %copy.8.bias_ref, f32[384,128]{1,0:T(8,128)S(1)} %get-tuple-element.23.own_tags_ref, f32[384,768]{1,0:T(8,128)S(1)} %get-tuple-element.26.caption_ref.unit_ref, f32[384,128]{1,0:T(8,128)S(1)} %get-tuple-element.42.scale_ref, ...), custom_call_target="tpu_custom_call" | custom-call | flops 1024 | bytes 1024 | tf_op jit(solution)/shard_map/pallas_call | solution.py:244
  (12 shorter events, 0.0 us)
Async XLA Ops:
  1.3 1.3 %copy-start = (f32[384,768]{1,0:T(8,128)S(1)}, f32[384,768]{1,0:T(8,128)}, u32[]{:S(2)}) copy-start(f32[384,768]{1,0:T(8,128)} %caption_ref.1) | copy-start | bytes 3538948
  2.6 2.5 %copy-start.1 = (f32[384,768]{1,0:T(8,128)S(1)}, f32[384,768]{1,0:T(8,128)}, u32[]{:S(2)}) copy-start(f32[384,768]{1,0:T(8,128)} %picture_ref.1) | copy-start | bytes 3538948
  2.7 38.6 %collective-permute-start.2 = (f32[392,768]{1,0:T(8,128)S(1)}, f32[392,768]{1,0:T(8,128)S(1)}, u32[]{:S(2)}, u32[]{:S(2)}) collective-permute-start(f32[392,768]{1,0:T(8,128)S(1)} %shard_map.68.staged_ref), channel_id=1, source_target_pairs={{0,256},{1,257},{2,258},{3,259},{4,260},{5,261},{6,262},{7,263},{8... | collective-permute-start | bytes 3612680 | tf_op jit(solution)/shard_map/ppermute | solution.py:23
  5.8 36.2 %collective-permute-start.1 = (f32[392,768]{1,0:T(8,128)S(1)}, f32[392,768]{1,0:T(8,128)S(1)}, u32[]{:S(2)}, u32[]{:S(2)}) collective-permute-start(f32[392,768]{1,0:T(8,128)S(1)} %get-tuple-element.32), channel_id=1, source_target_pairs={{0,1},{1,0},{2,3},{3,2},{4,5},{5,4},{6,7},{7,6},{8,9},{9,8},{10,11... | collective-permute-start | bytes 3612680 | tf_op jit(solution)/shard_map/ppermute | solution.py:23
  7.7 2.7 %collective-permute-start.9 = (f32[96,768]{1,0:T(8,128)S(1)}, f32[96,768]{1,0:T(8,128)S(1)}, u32[]{:S(2)}, u32[]{:S(2)}) collective-permute-start(f32[96,768]{1,0:T(8,128)S(1)} %get-tuple-element.40), channel_id=1, source_target_pairs={{127,252},{0,387},{255,380},{128,3},{383,508},{256,131},{511,124},... | collective-permute-start | bytes 884744 | tf_op jit(solution)/shard_map/ppermute | solution.py:47
  8.4 19.6 %collective-permute-start.5 = (f32[96,768]{1,0:T(8,128)S(1)}, f32[96,768]{1,0:T(8,128)S(1)}, u32[]{:S(2)}, u32[]{:S(2)}) collective-permute-start(f32[96,768]{1,0:T(8,128)S(1)} %get-tuple-element.38), channel_id=1, source_target_pairs={{127,224},{0,481},{255,352},{128,97},{383,480},{256,225},{511,96},... | collective-permute-start | bytes 884744 | tf_op jit(solution)/shard_map/ppermute | solution.py:47
  9.7 28.3 %collective-permute-start.3 = (f32[104,768]{1,0:T(8,128)S(1)}, f32[104,768]{1,0:T(8,128)S(1)}, u32[]{:S(2)}, u32[]{:S(2)}) collective-permute-start(f32[104,768]{1,0:T(8,128)S(1)} %get-tuple-element.37), channel_id=1, source_target_pairs={{127,158},{0,415},{255,286},{128,31},{383,414},{256,159},{511,30},... | collective-permute-start | bytes 958472 | tf_op jit(solution)/shard_map/ppermute | solution.py:47
  10.4 22.2 %collective-permute-start.7 = (f32[96,768]{1,0:T(8,128)S(1)}, f32[96,768]{1,0:T(8,128)S(1)}, u32[]{:S(2)}, u32[]{:S(2)}) collective-permute-start(f32[96,768]{1,0:T(8,128)S(1)} %get-tuple-element.39), channel_id=1, source_target_pairs={{127,222},{0,417},{255,350},{128,33},{383,478},{256,161},{511,94},... | collective-permute-start | bytes 884744 | tf_op jit(solution)/shard_map/ppermute | solution.py:47
  28.0 12.0 %collective-permute-start.10 = (f32[96,768]{1,0:T(8,128)S(1)}, f32[96,768]{1,0:T(8,128)S(1)}, u32[]{:S(2)}, u32[]{:S(2)}) collective-permute-start(f32[96,768]{1,0:T(8,128)S(1)} %collective-permute-done.9), channel_id=1, source_target_pairs={{124,0},{3,127},{252,128},{131,255},{380,256},{259,383},{508,384},... | collective-permute-start | bytes 884744 | tf_op jit(solution)/shard_map/ppermute | solution.py:57
  32.6 32.0 %collective-permute-start.11 = (f32[384,768]{1,0:T(8,128)S(1)}, f32[384,768]{1,0:T(8,128)S(1)}, u32[]{:S(2)}, u32[]{:S(2)}) collective-permute-start(f32[384,768]{1,0:T(8,128)S(1)} %get-tuple-element.24.picture_ref), channel_id=1, source_target_pairs={{0,256},{1,257},{2,258},{3,259},{4,260},{5,261},{6,262},{7,263},{8... | collective-permute-start | bytes 3538952 | tf_op jit(solution)/shard_map/ppermute | solution.py:23
  38.0 23.1 %collective-permute-start = (f32[392,768]{1,0:T(8,128)S(1)}, f32[392,768]{1,0:T(8,128)S(1)}, u32[]{:S(2)}, u32[]{:S(2)}) collective-permute-start(f32[392,768]{1,0:T(8,128)S(1)} %get-tuple-element.31), channel_id=1, source_target_pairs={{1,2},{2,1},{3,4},{4,3},{5,6},{6,5},{7,8},{8,7},{9,10},{10,9},{11,... | collective-permute-start | bytes 3612680 | tf_op jit(solution)/shard_map/ppermute | solution.py:23
  40.0 7.2 %collective-permute-start.6 = (f32[96,768]{1,0:T(8,128)S(1)}, f32[96,768]{1,0:T(8,128)S(1)}, u32[]{:S(2)}, u32[]{:S(2)}) collective-permute-start(f32[96,768]{1,0:T(8,128)S(1)} %collective-permute-done.5), channel_id=1, source_target_pairs={{96,0},{97,127},{224,128},{225,255},{352,256},{353,383},{480,384},... | collective-permute-start | bytes 884744 | tf_op jit(solution)/shard_map/ppermute | solution.py:57
  41.3 5.9 %collective-permute-start.8 = (f32[96,768]{1,0:T(8,128)S(1)}, f32[96,768]{1,0:T(8,128)S(1)}, u32[]{:S(2)}, u32[]{:S(2)}) collective-permute-start(f32[96,768]{1,0:T(8,128)S(1)} %collective-permute-done.7), channel_id=1, source_target_pairs={{94,0},{33,127},{222,128},{161,255},{350,256},{289,383},{478,384},... | collective-permute-start | bytes 884744 | tf_op jit(solution)/shard_map/ppermute | solution.py:57
  42.0 5.2 %collective-permute-start.4 = (f32[104,768]{1,0:T(8,128)S(1)}, f32[104,768]{1,0:T(8,128)S(1)}, u32[]{:S(2)}, u32[]{:S(2)}) collective-permute-start(f32[104,768]{1,0:T(8,128)S(1)} %collective-permute-done.3), channel_id=1, source_target_pairs={{30,0},{31,127},{158,128},{159,255},{286,256},{287,383},{414,384},... | collective-permute-start | bytes 958472 | tf_op jit(solution)/shard_map/ppermute | solution.py:57

commit v3 on v2

--- a/solution.py
+++ b/solution.py
@@ -12,6 +12,7 @@
 UP_BY = ((0, 15), (3, 0), (2, 15), (3, 14))
 DOWN_BY = ((0, 15), (3, 0), (1, 0), (0, 1))
 PARTS = len(UP_BY)
+BLOCKS = 3
 FAR_COST = 1 << 37
 VMEM = pl.BlockSpec(memory_space=pltpu.VMEM)
 SMEM = pl.BlockSpec(memory_space=pltpu.SMEM)
@@ -117,7 +118,7 @@
 
 def stage_kernel(caption_ref, tags_ref, out_ref):
     out_ref[: caption_ref.shape[0], :] = caption_ref[...]
-    put_tags(out_ref, tags_ref[...].astype(jnp.float32))
+    put_tags(out_ref, tags_ref[...].astype(jnp.float32).reshape(1, -1))
 
 
 def unit_kernel(
@@ -185,67 +186,79 @@
     return pull(own, halves(other_ref[:rows, :]), own_tags_ref[:, :1], tags, heat, bias)
 
 
-def core_kernel(
+def in_parts(place):
+    return jnp.logical_or(place == 0, place == PLANE - 1)
+
+
+def chip_kernel(
     heat_ref, bias_ref, own_tags_ref,
     caption_high_ref, caption_low_ref, picture_high_ref, picture_low_ref,
     other_ref, c_in_ref, p_in_ref, c_ref, p_ref,
 ):
     heat, bias = scalars(heat_ref, bias_ref)
+    even = is_even()
+    caption, picture = (caption_high_ref, caption_low_ref), (picture_high_ref, picture_low_ref)
+    more = near_pull(heat, bias, own_tags_ref, caption, picture, jnp.logical_not(even), other_ref)
+    more = jnp.where(in_parts(place_in_plane()), 0.0, more)
+    c_ref[...] = c_in_ref[...] + jnp.where(even, 0.0, more)
+    p_ref[...] = p_in_ref[...] + jnp.where(even, more, 0.0)
+
+
+def core_kernel(
+    heat_ref, bias_ref, own_tags_ref, picture_ref, scale_ref,
+    caption_high_ref, caption_low_ref, picture_high_ref, picture_low_ref,
+    other_ref, c_in_ref, p_in_ref, *refs,
+):
+    parts, (c_ref, p_ref, block) = refs[:PARTS], refs[PARTS:]
+    heat, bias = scalars(heat_ref, bias_ref)
+    rows = c_ref.shape[0]
+    step = rows // PARTS
     even = is_even()
     caption, picture = (caption_high_ref, caption_low_ref), (picture_high_ref, picture_low_ref)
     more = near_pull(heat, bias, own_tags_ref, caption, picture, even, other_ref)
     c_ref[...] = c_in_ref[...] + jnp.where(even, more, 0.0)
     p_ref[...] = p_in_ref[...] + jnp.where(even, 0.0, more)
 
-
-def chip_kernel(
-    heat_ref, bias_ref, own_tags_ref, picture_ref, scale_ref,
-    caption_high_ref, caption_low_ref, picture_high_ref, picture_low_ref,
-    other_ref, c_in_ref, p_in_ref, *refs,
-):
-    parts, (c_ref, p_ref, block) = refs[:PARTS], refs[PARTS:]
-    heat, bias = scalars(heat_ref, bias_ref)
-    rows = c_ref.shape[0]
-    step = rows // PARTS
-    even = is_even()
-    place = place_in_plane()
-    in_parts = jnp.logical_or(place == 0, place == PLANE - 1)
-
-    @pl.when(in_parts)
+    @pl.when(in_parts(place_in_plane()))
     def _():
         for k, part in enumerate(parts):
             block[k * step : (k + 1) * step, :] = part[:step, :]
         block[rows:, :] = parts[0][step:, :]
-
-    @pl.when(jnp.logical_not(in_parts))
-    def _():
-        block[...] = other_ref[...]
-
-    caption, picture = (caption_high_ref, caption_low_ref), (picture_high_ref, picture_low_ref)
-    more = near_pull(heat, bias, own_tags_ref, caption, picture, jnp.logical_not(even), block)
-    c_ref[...] = c_in_ref[...] + jnp.where(even, 0.0, more)
-    total = p_in_ref[...] + jnp.where(even, more, 0.0)
-    p_ref[...] = through_norm(total, picture_ref[...], scale_ref[:, :1], heat)
+        more = near_pull(heat, bias, own_tags_ref, caption, picture, jnp.logical_not(even), block)
+        c_ref[...] += jnp.where(even, 0.0, more)
+        p_ref[...] += jnp.where(even, more, 0.0)
+
+    p_ref[...] = through_norm(p_ref[...], picture_ref[...], scale_ref[:, :1], heat)
 
 
 def last_kernel(
     heat_ref, bias_ref, own_tags_ref, unit_ref, scale_ref, high_ref, low_ref, far_ref, tags_ref,
-    in_ref, out_ref,
-):
-    heat, bias = scalars(heat_ref, bias_ref)
-    rows = out_ref.shape[0]
+    in_ref, out_ref, block, sem,
+):
+    heat, bias = scalars(heat_ref, bias_ref)
+    rows = block.shape[0]
     own, other = (high_ref[...], low_ref[...]), halves(far_ref[...])
     tags = tags_ref[rows : rows + 1, :rows]
-    total = in_ref[...] + pull(own, other, own_tags_ref[:, :1], tags, heat, bias)
-    out_ref[...] = through_norm(total, unit_ref[...], scale_ref[:, :1], heat)
-
-
-def call(kernel, out_shape, *operands, cost=1024, scratch=()):
+    slope = halves(slopes(own, other, own_tags_ref[:, :1], tags, heat, bias))
+    step = rows // BLOCKS
+    copies = []
+    for k in range(BLOCKS):
+        at = pl.ds(k * step, step)
+        part = [half[k * step : (k + 1) * step] for half in slope]
+        total = in_ref[at, :] + dot_nn(part, other)
+        block[at, :] = through_norm(total, unit_ref[at, :], scale_ref[at, :1], heat)
+        copies.append(pltpu.make_async_copy(block.at[at, :], out_ref.at[at, :], sem.at[k]))
+        copies[-1].start()
+    for copy in copies:
+        copy.wait()
+
+
+def call(kernel, out_shape, *operands, cost=1024, scratch=(), hbm_out=False):
     return pl.pallas_call(
         kernel,
         out_shape=out_shape,
         in_specs=[SMEM if x.size == 1 else VMEM for x in operands],
-        out_specs=[VMEM] * len(out_shape),
+        out_specs=[pl.BlockSpec(memory_space=pltpu.HBM) if hbm_out else VMEM] * len(out_shape),
         scratch_shapes=scratch,
         compiler_params=pltpu.CompilerParams(vmem_limit_bytes=24 * 1024 * 1024),
         cost_estimate=pl.CostEstimate(flops=cost, bytes_accessed=1024, transcendentals=0),
@@ -266,7 +279,7 @@
     def over_half(i):
         return i + count // 2
 
-    (staged,) = call(stage_kernel, [f32(rows + 8)], caption, tags[None, :])
+    (staged,) = call(stage_kernel, [f32(rows + 8)], caption, tags)
     far_caption = swap(staged, over_half)
     caption, picture, core, chip, own_tags, caption_scale, picture_scale, *parts = call(
         unit_kernel,
@@ -284,15 +297,17 @@
         own_kernel, [b16(rows)] * 4 + [f32(rows)] * 2, *scalar, staged, caption, picture
     )
     (p,) = call(far_kernel, [f32(rows)], *scalar, *units[2:], far_caption, p, cost=FAR_COST)
-    c, p = call(core_kernel, [f32(rows)] * 2, *scalar, *units, core, c, p)
+    c, p = call(chip_kernel, [f32(rows)] * 2, *scalar, *units, chip, c, p)
     c, p = call(
-        chip_kernel, [f32(rows)] * 2,
-        *scalar, picture, picture_scale, *units, chip, c, p, *parts,
+        core_kernel, [f32(rows)] * 2,
+        *scalar, picture, picture_scale, *units, core, c, p, *parts,
         scratch=[pltpu.VMEM((rows + 8, width), jnp.float32)],
     )
     (c,) = call(
         last_kernel, [f32(rows)],
         *scalar, caption, caption_scale, *units[:2], far_picture, far_caption, c,
+        scratch=[pltpu.VMEM((rows, width), jnp.float32), pltpu.SemaphoreType.DMA((BLOCKS,))],
+        hbm_out=True,
     )
     return p, c
 

time: 68.5 us -> 67.3 us (0.982)
  the two profiles are of different devices: /device:TPU:22 before, /device:TPU:488 now
where the time goes in v3:
time: 67.3 us; the launch traced here: 66.9 us
  waiting for transfers between devices  30.2 us (45%)
  starting transfers between devices  18 us (27%)
  Pallas kernels  14.5 us (22%)
  between operations  2.15 us (3%)
  local copies, waits for them, and re-layouts  2.04 us (3%)
    ppermute x4, waiting for transfers between devices, swap(): lax.ppermute(block, 'dp', [pair for pair in route if pair[0] != pair[1]])  26.8 us
    pallas_call x7, Pallas kernels, call(): pl.pallas_call(kernel, out_shape=out_shape, in_specs=[SMEM if x.size == 1...  14.5 us
    ppermute x4, starting transfers between devices, swap(): lax.ppermute(block, 'dp', [pair for pair in route if pair[0] != pair[1]])  11.3 us
    ppermute x4, waiting for transfers between devices, outward(): return lax.ppermute(block, 'dp', route)  3.35 us
    ppermute x4, starting transfers between devices, homeward(): return lax.ppermute(block, 'dp', route)  3.34 us
    ppermute x4, starting transfers between devices, outward(): return lax.ppermute(block, 'dp', route)  3.33 us
    unnamed x6, local copies, waits for them, and re-layouts  2.04 us
  transfers between devices with their start and end apart: 12, of which 3 were waited for; matrix products, arithmetic and copies ran while one was open for 0% of the time, Pallas kernels for 17%

profile of v3, /device:TPU:488, one launch (start us, length us, event | category | flops | bytes accessed | tf_op | source)
XLA Modules:
  0.0 66.9 jit_solution(6029624578449427027)
XLA Ops:
  0.6 1.4 %copy-done.1 = f32[384,768]{1,0:T(8,128)S(1)} copy-done((f32[384,768]{1,0:T(8,128)S(1)}, f32[384,768]{1,0:T(8,128)}, u32[]{:S(2)}) %copy-start.1) | copy-done | bytes 1179672
  2.0 0.7 %copy-done.2 = s32[384]{0:T(512)S(1)} copy-done((s32[384]{0:T(512)S(1)}, s32[384]{0:T(512)}, u32[]{:S(2)}) %copy-start.2) | copy-done | bytes 1560
  2.7 0.1 shard_map.68.staged_ref
  2.8 4.2 %collective-permute-start.2 = (f32[392,768]{1,0:T(8,128)S(1)}, f32[392,768]{1,0:T(8,128)S(1)}, u32[]{:S(2)}, u32[]{:S(2)}) collective-permute-start(f32[392,768]{1,0:T(8,128)S(1)} %shard_map.68.staged_ref), channel_id=1, source_target_pairs={{0,256},{1,257},{2,258},{3,259},{4,260},{5,261},{6,262},{7,263},{8... | collective-permute-start | bytes 3612680 | tf_op jit(solution)/shard_map/ppermute | solution.py:24
  7.0 0.7 %shard_map.69 = (f32[384,768]{1,0:T(8,128)S(1)}, f32[384,768]{1,0:T(8,128)S(1)}, f32[392,768]{1,0:T(8,128)S(1)}, f32[392,768]{1,0:T(8,128)S(1)}, f32[384,128]{1,...) custom-call(f32[392,768]{1,0:T(8,128)S(1)} %shard_map.68.staged_ref,, ...), custom_call_target="tpu_custom_call" | custom-call | flops 1024 | bytes 1024 | tf_op jit(solution)/shard_map/pallas_call | solution.py:257
  7.7 2.1 %collective-permute-start.1 = (f32[392,768]{1,0:T(8,128)S(1)}, f32[392,768]{1,0:T(8,128)S(1)}, u32[]{:S(2)}, u32[]{:S(2)}) collective-permute-start(f32[392,768]{1,0:T(8,128)S(1)} %get-tuple-element.32), channel_id=1, source_target_pairs={{1,2},{2,1},{3,4},{4,3},{5,6},{6,5},{7,8},{8,7},{9,10},{10,9},{11,... | collective-permute-start | bytes 3612680 | tf_op jit(solution)/shard_map/ppermute | solution.py:24
  9.8 0.7 %collective-permute-start.9 = (f32[96,768]{1,0:T(8,128)S(1)}, f32[96,768]{1,0:T(8,128)S(1)}, u32[]{:S(2)}, u32[]{:S(2)}) collective-permute-start(f32[96,768]{1,0:T(8,128)S(1)} %get-tuple-element.40), channel_id=1, source_target_pairs={{127,252},{0,387},{255,380},{128,3},{383,508},{256,131},{511,124},... | collective-permute-start | bytes 884744 | tf_op jit(solution)/shard_map/ppermute | solution.py:48
  10.5 0.7 %collective-permute-start.5 = (f32[96,768]{1,0:T(8,128)S(1)}, f32[96,768]{1,0:T(8,128)S(1)}, u32[]{:S(2)}, u32[]{:S(2)}) collective-permute-start(f32[96,768]{1,0:T(8,128)S(1)} %get-tuple-element.38), channel_id=1, source_target_pairs={{127,224},{0,481},{255,352},{128,97},{383,480},{256,225},{511,96},... | collective-permute-start | bytes 884744 | tf_op jit(solution)/shard_map/ppermute | solution.py:48
  11.2 1.3 %collective-permute-start.3 = (f32[104,768]{1,0:T(8,128)S(1)}, f32[104,768]{1,0:T(8,128)S(1)}, u32[]{:S(2)}, u32[]{:S(2)}) collective-permute-start(f32[104,768]{1,0:T(8,128)S(1)} %get-tuple-element.37), channel_id=1, source_target_pairs={{127,158},{0,415},{255,286},{128,31},{383,414},{256,159},{511,30},... | collective-permute-start | bytes 958472 | tf_op jit(solution)/shard_map/ppermute | solution.py:48
  12.5 0.7 %collective-permute-start.7 = (f32[96,768]{1,0:T(8,128)S(1)}, f32[96,768]{1,0:T(8,128)S(1)}, u32[]{:S(2)}, u32[]{:S(2)}) collective-permute-start(f32[96,768]{1,0:T(8,128)S(1)} %get-tuple-element.39), channel_id=1, source_target_pairs={{127,222},{0,417},{255,350},{128,33},{383,478},{256,161},{511,94},... | collective-permute-start | bytes 884744 | tf_op jit(solution)/shard_map/ppermute | solution.py:48
  13.2 0.7 %collective-permute-start.10 = (f32[96,768]{1,0:T(8,128)S(1)}, f32[96,768]{1,0:T(8,128)S(1)}, u32[]{:S(2)}, u32[]{:S(2)}) collective-permute-start(f32[96,768]{1,0:T(8,128)S(1)} %collective-permute-done.9), channel_id=1, source_target_pairs={{124,0},{3,127},{252,128},{131,255},{380,256},{259,383},{508,384},... | collective-permute-start | bytes 884744 | tf_op jit(solution)/shard_map/ppermute | solution.py:58
  15.1 2.7 %shard_map.70 = (bf16[384,768]{1,0:T(8,128)(2,1)S(1)}, bf16[384,768]{1,0:T(8,128)(2,1)S(1)}, bf16[384,768]{1,0:T(8,128)(2,1)S(1)}, bf16[384,768]{1,0:T(8,128)(2,...) custom-call(f32[1]{0:T(128)S(6)} %copy.7.heat_ref, f32[1]{0:T(128)S(6)} %copy.8.bias_ref, ...), custom_call_target="tpu_custom_call" | custom-call | flops 1024 | bytes 1024 | tf_op jit(solution)/shard_map/pallas_call | solution.py:257
  17.8 3.1 %collective-permute-start.11 = (f32[384,768]{1,0:T(8,128)S(1)}, f32[384,768]{1,0:T(8,128)S(1)}, u32[]{:S(2)}, u32[]{:S(2)}) collective-permute-start(f32[384,768]{1,0:T(8,128)S(1)} %get-tuple-element.24.picture_ref), channel_id=1, source_target_pairs={{0,256},{1,257},{2,258},{3,259},{4,260},{5,261},{6,262},{7,263},{8... | collective-permute-start | bytes 3538952 | tf_op jit(solution)/shard_map/ppermute | solution.py:24
  21.0 3.3 %collective-permute-done.3 = f32[104,768]{1,0:T(8,128)S(1)} collective-permute-done((f32[104,768]{1,0:T(8,128)S(1)}, f32[104,768]{1,0:T(8,128)S(1)}, u32[]{:S(2)}, u32[]{:S(2)}) %collective-permute-start.3) | collective-permute-done | bytes 319520 | tf_op jit(solution)/shard_map/ppermute | solution.py:48
  24.3 1.9 %collective-permute-start = (f32[392,768]{1,0:T(8,128)S(1)}, f32[392,768]{1,0:T(8,128)S(1)}, u32[]{:S(2)}, u32[]{:S(2)}) collective-permute-start(f32[392,768]{1,0:T(8,128)S(1)} %get-tuple-element.31), channel_id=1, source_target_pairs={{0,1},{1,0},{2,3},{3,2},{4,5},{5,4},{6,7},{7,6},{8,9},{9,8},{10,11... | collective-permute-start | bytes 3612680 | tf_op jit(solution)/shard_map/ppermute | solution.py:24
  26.2 0.7 %collective-permute-start.6 = (f32[96,768]{1,0:T(8,128)S(1)}, f32[96,768]{1,0:T(8,128)S(1)}, u32[]{:S(2)}, u32[]{:S(2)}) collective-permute-start(f32[96,768]{1,0:T(8,128)S(1)} %collective-permute-done.5), channel_id=1, source_target_pairs={{96,0},{97,127},{224,128},{225,255},{352,256},{353,383},{480,384},... | collective-permute-start | bytes 884744 | tf_op jit(solution)/shard_map/ppermute | solution.py:58
  26.9 12.9 %collective-permute-done.2.far_ref.tags_ref = f32[392,768]{1,0:T(8,128)S(1)} collective-permute-done((f32[392,768]{1,0:T(8,128)S(1)}, f32[392,768]{1,0:T(8,128)S(1)}, u32[]{:S(2)}, u32[]{:S(2)}) %collective-permute-start.2) | collective-permute-done | bytes 1204256 | tf_op jit(solution)/shard_map/ppermute | solution.py:24
  39.8 0.7 collective-permute-start.8
  40.5 1.3 %collective-permute-start.4 = (f32[104,768]{1,0:T(8,128)S(1)}, f32[104,768]{1,0:T(8,128)S(1)}, u32[]{:S(2)}, u32[]{:S(2)}) collective-permute-start(f32[104,768]{1,0:T(8,128)S(1)} %collective-permute-done.3), channel_id=1, source_target_pairs={{30,0},{31,127},{158,128},{159,255},{286,256},{287,383},{414,384},... | collective-permute-start | bytes 958472 | tf_op jit(solution)/shard_map/ppermute | solution.py:58
  41.8 2.3 %shard_map.71.p_in_ref = f32[384,768]{1,0:T(8,128)S(1)} custom-call(f32[1]{0:T(128)S(6)} %copy.7.heat_ref, f32[1]{0:T(128)S(6)} %copy.8.bias_ref, f32[384,128]{1,0:T(8,128)S(1)} %get-tuple-element.23.own_tags_ref, bf16[384,768]{1,0:T(8,128)(2,1)S(1)} %get-tuple-element.29.high_ref.picture_high_ref, ...), custom_call_target="tpu_custom_call" | custom-call | flops 137438953472 | bytes 1024 | tf_op jit(solution)/shard_map/pallas_call | solution.py:257
  44.1 2.2 %shard_map.72 = (f32[384,768]{1,0:T(8,128)S(1)}, f32[384,768]{1,0:T(8,128)S(1)}) custom-call(f32[1]{0:T(128)S(6)} %copy.7.heat_ref, f32[1]{0:T(128)S(6)} %copy.8.bias_ref, f32[384,128]{1,0:T(8,128)S(1)} %get-tuple-element.23.own_tags_ref, bf16[384,768]{1,0:T(8,128)(2,1)S(1)} %get-tuple-element.27.caption_high_ref.high_ref, ...), custom_call_target="tpu_custom_call" | custom-call | flops 1024 | bytes 1024 | tf_op jit(solution)/shard_map/pallas_call | solution.py:257
  46.4 3.7 %shard_map.73 = (f32[384,768]{1,0:T(8,128)S(1)}, f32[384,768]{1,0:T(8,128)}) custom-call(f32[1]{0:T(128)S(6)} %copy.7.heat_ref, f32[1]{0:T(128)S(6)} %copy.8.bias_ref, f32[384,128]{1,0:T(8,128)S(1)} %get-tuple-element.23.own_tags_ref, f32[384,768]{1,0:T(8,128)S(1)} %get-tuple-element.24.picture_ref, f32[384,128]{1,0:T(8,128)S(1)} %get-tuple-element.25.scale_ref, ...), custom_call_target="tpu_custom_call" | custom-call | flops 1024 | bytes 1024 | tf_op jit(solution)/shard_map/pallas_call | solution.py:257
  50.0 13.9 %collective-permute-done.11.far_ref = f32[384,768]{1,0:T(8,128)S(1)} collective-permute-done((f32[384,768]{1,0:T(8,128)S(1)}, f32[384,768]{1,0:T(8,128)S(1)}, u32[]{:S(2)}, u32[]{:S(2)}) %collective-permute-start.11) | collective-permute-done | bytes 1179680 | tf_op jit(solution)/shard_map/ppermute | solution.py:24
  64.0 2.9 %shard_map.74 = f32[384,768]{1,0:T(8,128)} custom-call(f32[1]{0:T(128)S(6)} %copy.7.heat_ref, f32[1]{0:T(128)S(6)} %copy.8.bias_ref, f32[384,128]{1,0:T(8,128)S(1)} %get-tuple-element.23.own_tags_ref, f32[384,768]{1,0:T(8,128)S(1)} %get-tuple-element.26.caption_ref.unit_ref, f32[384,128]{1,0:T(8,128)S(1)} %get-tuple-element.42.scale_ref, ...), custom_call_target="tpu_custom_call" | custom-call | flops 1024 | bytes 1024 | tf_op jit(solution)/shard_map/pallas_call | solution.py:257
  (13 shorter events, 0.0 us)
Async XLA Ops:
  0.6 6.4 %copy-start = (f32[384,768]{1,0:T(8,128)S(1)}, f32[384,768]{1,0:T(8,128)}, u32[]{:S(2)}) copy-start(f32[384,768]{1,0:T(8,128)} %picture_ref.1) | copy-start | bytes 3538948
  0.6 1.4 %copy-start.1 = (f32[384,768]{1,0:T(8,128)S(1)}, f32[384,768]{1,0:T(8,128)}, u32[]{:S(2)}) copy-start(f32[384,768]{1,0:T(8,128)} %caption_ref.1) | copy-start | bytes 3538948
  2.0 0.7 %copy-start.2 = (s32[384]{0:T(512)S(1)}, s32[384]{0:T(512)}, u32[]{:S(2)}) copy-start(s32[384]{0:T(512)} %tags_ref.1) | copy-start | bytes 4612
  2.8 37.0 %collective-permute-start.2 = (f32[392,768]{1,0:T(8,128)S(1)}, f32[392,768]{1,0:T(8,128)S(1)}, u32[]{:S(2)}, u32[]{:S(2)}) collective-permute-start(f32[392,768]{1,0:T(8,128)S(1)} %shard_map.68.staged_ref), channel_id=1, source_target_pairs={{0,256},{1,257},{2,258},{3,259},{4,260},{5,261},{6,262},{7,263},{8... | collective-permute-start | bytes 3612680 | tf_op jit(solution)/shard_map/ppermute | solution.py:24
  7.7 32.8 %collective-permute-start.1 = (f32[392,768]{1,0:T(8,128)S(1)}, f32[392,768]{1,0:T(8,128)S(1)}, u32[]{:S(2)}, u32[]{:S(2)}) collective-permute-start(f32[392,768]{1,0:T(8,128)S(1)} %get-tuple-element.32), channel_id=1, source_target_pairs={{1,2},{2,1},{3,4},{4,3},{5,6},{6,5},{7,8},{8,7},{9,10},{10,9},{11,... | collective-permute-start | bytes 3612680 | tf_op jit(solution)/shard_map/ppermute | solution.py:24
  9.8 2.7 %collective-permute-start.9 = (f32[96,768]{1,0:T(8,128)S(1)}, f32[96,768]{1,0:T(8,128)S(1)}, u32[]{:S(2)}, u32[]{:S(2)}) collective-permute-start(f32[96,768]{1,0:T(8,128)S(1)} %get-tuple-element.40), channel_id=1, source_target_pairs={{127,252},{0,387},{255,380},{128,3},{383,508},{256,131},{511,124},... | collective-permute-start | bytes 884744 | tf_op jit(solution)/shard_map/ppermute | solution.py:48
  10.5 2.7 %collective-permute-start.5 = (f32[96,768]{1,0:T(8,128)S(1)}, f32[96,768]{1,0:T(8,128)S(1)}, u32[]{:S(2)}, u32[]{:S(2)}) collective-permute-start(f32[96,768]{1,0:T(8,128)S(1)} %get-tuple-element.38), channel_id=1, source_target_pairs={{127,224},{0,481},{255,352},{128,97},{383,480},{256,225},{511,96},... | collective-permute-start | bytes 884744 | tf_op jit(solution)/shard_map/ppermute | solution.py:48
  11.2 13.2 %collective-permute-start.3 = (f32[104,768]{1,0:T(8,128)S(1)}, f32[104,768]{1,0:T(8,128)S(1)}, u32[]{:S(2)}, u32[]{:S(2)}) collective-permute-start(f32[104,768]{1,0:T(8,128)S(1)} %get-tuple-element.37), channel_id=1, source_target_pairs={{127,158},{0,415},{255,286},{128,31},{383,414},{256,159},{511,30},... | collective-permute-start | bytes 958472 | tf_op jit(solution)/shard_map/ppermute | solution.py:48
  12.5 5.3 %collective-permute-start.7 = (f32[96,768]{1,0:T(8,128)S(1)}, f32[96,768]{1,0:T(8,128)S(1)}, u32[]{:S(2)}, u32[]{:S(2)}) collective-permute-start(f32[96,768]{1,0:T(8,128)S(1)} %get-tuple-element.39), channel_id=1, source_target_pairs={{127,222},{0,417},{255,350},{128,33},{383,478},{256,161},{511,94},... | collective-permute-start | bytes 884744 | tf_op jit(solution)/shard_map/ppermute | solution.py:48
  13.2 13.1 %collective-permute-start.10 = (f32[96,768]{1,0:T(8,128)S(1)}, f32[96,768]{1,0:T(8,128)S(1)}, u32[]{:S(2)}, u32[]{:S(2)}) collective-permute-start(f32[96,768]{1,0:T(8,128)S(1)} %collective-permute-done.9), channel_id=1, source_target_pairs={{124,0},{3,127},{252,128},{131,255},{380,256},{259,383},{508,384},... | collective-permute-start | bytes 884744 | tf_op jit(solution)/shard_map/ppermute | solution.py:58
  17.8 46.1 %collective-permute-start.11 = (f32[384,768]{1,0:T(8,128)S(1)}, f32[384,768]{1,0:T(8,128)S(1)}, u32[]{:S(2)}, u32[]{:S(2)}) collective-permute-start(f32[384,768]{1,0:T(8,128)S(1)} %get-tuple-element.24.picture_ref), channel_id=1, source_target_pairs={{0,256},{1,257},{2,258},{3,259},{4,260},{5,261},{6,262},{7,263},{8... | collective-permute-start | bytes 3538952 | tf_op jit(solution)/shard_map/ppermute | solution.py:24
  24.3 22.1 %collective-permute-start = (f32[392,768]{1,0:T(8,128)S(1)}, f32[392,768]{1,0:T(8,128)S(1)}, u32[]{:S(2)}, u32[]{:S(2)}) collective-permute-start(f32[392,768]{1,0:T(8,128)S(1)} %get-tuple-element.31), channel_id=1, source_target_pairs={{0,1},{1,0},{2,3},{3,2},{4,5},{5,4},{6,7},{7,6},{8,9},{9,8},{10,11... | collective-permute-start | bytes 3612680 | tf_op jit(solution)/shard_map/ppermute | solution.py:24
  26.2 20.1 %collective-permute-start.6 = (f32[96,768]{1,0:T(8,128)S(1)}, f32[96,768]{1,0:T(8,128)S(1)}, u32[]{:S(2)}, u32[]{:S(2)}) collective-permute-start(f32[96,768]{1,0:T(8,128)S(1)} %collective-permute-done.5), channel_id=1, source_target_pairs={{96,0},{97,127},{224,128},{225,255},{352,256},{353,383},{480,384},... | collective-permute-start | bytes 884744 | tf_op jit(solution)/shard_map/ppermute | solution.py:58
  39.8 6.5 %collective-permute-start.8 = (f32[96,768]{1,0:T(8,128)S(1)}, f32[96,768]{1,0:T(8,128)S(1)}, u32[]{:S(2)}, u32[]{:S(2)}) collective-permute-start(f32[96,768]{1,0:T(8,128)S(1)} %collective-permute-done.7), channel_id=1, source_target_pairs={{94,0},{33,127},{222,128},{161,255},{350,256},{289,383},{478,384},... | collective-permute-start | bytes 884744 | tf_op jit(solution)/shard_map/ppermute | solution.py:58
  40.5 5.9 %collective-permute-start.4 = (f32[104,768]{1,0:T(8,128)S(1)}, f32[104,768]{1,0:T(8,128)S(1)}, u32[]{:S(2)}, u32[]{:S(2)}) collective-permute-start(f32[104,768]{1,0:T(8,128)S(1)} %collective-permute-done.3), channel_id=1, source_target_pairs={{30,0},{31,127},{158,128},{159,255},{286,256},{287,383},{414,384},... | collective-permute-start | bytes 958472 | tf_op jit(solution)/shard_map/ppermute | solution.py:58

commit v4 on v3

--- a/solution.py
+++ b/solution.py
@@ -13,6 +13,7 @@
 DOWN_BY = ((0, 15), (3, 0), (1, 0), (0, 1))
 PARTS = len(UP_BY)
 BLOCKS = 3
+STAGES = 4
 FAR_COST = 1 << 37
 VMEM = pl.BlockSpec(memory_space=pltpu.VMEM)
 SMEM = pl.BlockSpec(memory_space=pltpu.SMEM)
@@ -116,24 +117,38 @@
     return lax.rem(lax.axis_index("dp"), 2) == 0
 
 
-def stage_kernel(caption_ref, tags_ref, out_ref):
-    out_ref[: caption_ref.shape[0], :] = caption_ref[...]
-    put_tags(out_ref, tags_ref[...].astype(jnp.float32).reshape(1, -1))
+def stage_kernel(caption_ref, tags_ref, out_ref, tags, sem):
+    rows = caption_ref.shape[0]
+    copies = [pltpu.make_async_copy(tags_ref, tags, sem.at[STAGES])]
+    for k in range(STAGES):
+        at = pl.ds(k * (rows // STAGES), rows // STAGES)
+        copies.append(pltpu.make_async_copy(caption_ref.at[at, :], out_ref.at[at, :], sem.at[k]))
+    for copy in copies:
+        copy.start()
+    copies[0].wait()
+    put_tags(out_ref, tags[...].astype(jnp.float32).reshape(1, -1))
+    for copy in copies[1:]:
+        copy.wait()
 
 
 def unit_kernel(
     staged_ref, picture_ref,
-    caption_out, picture_out, core_out, chip_out, own_tags_out, caption_scale, picture_scale, *parts,
-):
+    caption_out, picture_out, core_out, chip_out, own_tags_out, caption_scale, picture_scale, *refs,
+):
+    parts, (raw, sem) = refs[:PARTS], refs[PARTS:]
     rows = picture_ref.shape[0]
+    copy = pltpu.make_async_copy(picture_ref, raw, sem)
+    copy.start()
     even = is_even()
     tags = staged_ref[rows : rows + 1, :rows]
     own_tags_out[...] = jnp.broadcast_to(column_of(tags), own_tags_out.shape)
     units = []
     for source, out, scale_out in (
         (staged_ref, caption_out, caption_scale),
-        (picture_ref, picture_out, picture_scale),
+        (raw, picture_out, picture_scale),
     ):
+        if source is raw:
+            copy.wait()
         value = source[:rows, :]
         scale = inverse_norm(value)
         units.append(value * scale)
@@ -279,14 +294,27 @@
     def over_half(i):
         return i + count // 2
 
-    (staged,) = call(stage_kernel, [f32(rows + 8)], caption, tags)
+    hbm = pl.BlockSpec(memory_space=pltpu.HBM)
+    staged = pl.pallas_call(
+        stage_kernel,
+        out_shape=f32(rows + 8),
+        in_specs=[hbm, hbm],
+        out_specs=VMEM,
+        scratch_shapes=[pltpu.VMEM(tags.shape, jnp.int32), pltpu.SemaphoreType.DMA((STAGES + 1,))],
+        cost_estimate=pl.CostEstimate(flops=1024, bytes_accessed=1024, transcendentals=0),
+        compiler_params=pltpu.CompilerParams(vmem_limit_bytes=24 * 1024 * 1024),
+    )(*(pltpu.with_memory_space_constraint(x, pltpu.HBM) for x in (caption, tags)))
     far_caption = swap(staged, over_half)
-    caption, picture, core, chip, own_tags, caption_scale, picture_scale, *parts = call(
+    caption, picture, core, chip, own_tags, caption_scale, picture_scale, *parts = pl.pallas_call(
         unit_kernel,
-        [f32(rows)] * 2 + [f32(rows + 8)] * 2 + [f32(rows, 128)] * 3
+        out_shape=[f32(rows)] * 2 + [f32(rows + 8)] * 2 + [f32(rows, 128)] * 3
         + [f32(step + 8)] + [f32(step)] * (PARTS - 1),
-        staged, picture,
-    )
+        in_specs=[VMEM, hbm],
+        out_specs=[VMEM] * (7 + PARTS),
+        scratch_shapes=[pltpu.VMEM((rows, width), jnp.float32), pltpu.SemaphoreType.DMA(())],
+        cost_estimate=pl.CostEstimate(flops=1024, bytes_accessed=1024, transcendentals=0),
+        compiler_params=pltpu.CompilerParams(vmem_limit_bytes=24 * 1024 * 1024),
+    )(staged, pltpu.with_memory_space_constraint(picture, pltpu.HBM))
     parts = [outward(part, k) for k, part in enumerate(parts)]
     parts = [homeward(part, k) for k, part in enumerate(parts)]
     core = swap(core, over_core)

time: 67.3 us -> 66.4 us (0.987)
  local copies, waits for them, and re-layouts: 2.04 us -> 0 us
  Pallas kernels: 14.5 us -> 16.5 us
  waiting for transfers between devices: 30.2 us -> 29.3 us
    pallas_call x0 -> x2, Pallas kernels: none -> 2.98 us  [the longest x1 1.69 us: local(): pl.pallas_call(unit_kernel, out_shape=[f32(rows)] * 2 + [f32(rows + 8)] *...]
    unnamed x6 -> x0, local copies, waits for them, and re-layouts: 2.04 us -> none
    pallas_call x7 -> x5, Pallas kernels: 14.5 us -> 13.5 us  [call(): pl.pallas_call(kernel, out_shape=out_shape, in_specs=[SMEM if x.size == 1...]
    ppermute x4, waiting for transfers between devices: 26.8 us -> 25.9 us  [swap(): lax.ppermute(block, 'dp', [pair for pair in route if pair[0] != pair[1]])]
  transfers between devices with their start and end apart: 12 -> 12, of which waited for: 3 -> 3; matrix products, arithmetic and copies ran while one was open for 0% -> 0% of each run, Pallas kernels for 17% -> 19%
where the time goes in v4:
time: 66.4 us; the launch traced here: 65.9 us
  waiting for transfers between devices  29.3 us (44%)
  starting transfers between devices  18 us (27%)
  Pallas kernels  16.5 us (25%)
  between operations  2.13 us (3%)
    ppermute x4, waiting for transfers between devices, swap(): lax.ppermute(block, 'dp', [pair for pair in route if pair[0] != pair[1]])  25.9 us
    pallas_call x5, Pallas kernels, call(): pl.pallas_call(kernel, out_shape=out_shape, in_specs=[SMEM if x.size == 1...  13.5 us
    ppermute x4, starting transfers between devices, swap(): lax.ppermute(block, 'dp', [pair for pair in route if pair[0] != pair[1]])  11.3 us
    ppermute x4, waiting for transfers between devices, outward(): return lax.ppermute(block, 'dp', route)  3.4 us
    ppermute x4, starting transfers between devices, homeward(): return lax.ppermute(block, 'dp', route)  3.34 us
    ppermute x4, starting transfers between devices, outward(): return lax.ppermute(block, 'dp', route)  3.33 us
    pallas_call x1, Pallas kernels, local(): pl.pallas_call(unit_kernel, out_shape=[f32(rows)] * 2 + [f32(rows + 8)] *...  1.69 us
  transfers between devices with their start and end apart: 12, of which 3 were waited for; matrix products, arithmetic and copies ran while one was open for 0% of the time, Pallas kernels for 19%

profile of v4, /device:TPU:488, one launch (start us, length us, event | category | flops | bytes accessed | tf_op | source)
XLA Modules:
  0.0 65.9 jit_solution(11747428632323226203)
XLA Ops:
  0.6 1.3 %shard_map.68.staged_ref = f32[392,768]{1,0:T(8,128)S(1)} custom-call(f32[384,768]{1,0:T(8,128)} %caption_ref.1, s32[384]{0:T(512)} %tags_ref.1), custom_call_target="tpu_custom_call" | custom-call | flops 1024 | bytes 1024 | tf_op jit(solution)/shard_map/pallas_call | solution.py:298
  1.9 4.2 %collective-permute-start.2 = (f32[392,768]{1,0:T(8,128)S(1)}, f32[392,768]{1,0:T(8,128)S(1)}, u32[]{:S(2)}, u32[]{:S(2)}) collective-permute-start(f32[392,768]{1,0:T(8,128)S(1)} %shard_map.68.staged_ref), channel_id=1, source_target_pairs={{0,256},{1,257},{2,258},{3,259},{4,260},{5,261},{6,262},{7,263},{8... | collective-permute-start | bytes 3612680 | tf_op jit(solution)/shard_map/ppermute | solution.py:25
  6.1 1.7 %shard_map.69 = (f32[384,768]{1,0:T(8,128)S(1)}, f32[384,768]{1,0:T(8,128)S(1)}, f32[392,768]{1,0:T(8,128)S(1)}, f32[392,768]{1,0:T(8,128)S(1)}, f32[384,128]{1,...) custom-call(f32[392,768]{1,0:T(8,128)S(1)} %shard_map.68.staged_ref,, ...), custom_call_target="tpu_custom_call" | custom-call | flops 1024 | bytes 1024 | tf_op jit(solution)/shard_map/pallas_call | solution.py:308
  7.8 2.1 %collective-permute-start.1 = (f32[392,768]{1,0:T(8,128)S(1)}, f32[392,768]{1,0:T(8,128)S(1)}, u32[]{:S(2)}, u32[]{:S(2)}) collective-permute-start(f32[392,768]{1,0:T(8,128)S(1)} %get-tuple-element.32), channel_id=1, source_target_pairs={{1,2},{2,1},{3,4},{4,3},{5,6},{6,5},{7,8},{8,7},{9,10},{10,9},{11,... | collective-permute-start | bytes 3612680 | tf_op jit(solution)/shard_map/ppermute | solution.py:25
  9.9 0.7 %collective-permute-start.9 = (f32[96,768]{1,0:T(8,128)S(1)}, f32[96,768]{1,0:T(8,128)S(1)}, u32[]{:S(2)}, u32[]{:S(2)}) collective-permute-start(f32[96,768]{1,0:T(8,128)S(1)} %get-tuple-element.40), channel_id=1, source_target_pairs={{127,252},{0,387},{255,380},{128,3},{383,508},{256,131},{511,124},... | collective-permute-start | bytes 884744 | tf_op jit(solution)/shard_map/ppermute | solution.py:49
  10.6 0.7 %collective-permute-start.5 = (f32[96,768]{1,0:T(8,128)S(1)}, f32[96,768]{1,0:T(8,128)S(1)}, u32[]{:S(2)}, u32[]{:S(2)}) collective-permute-start(f32[96,768]{1,0:T(8,128)S(1)} %get-tuple-element.38), channel_id=1, source_target_pairs={{127,224},{0,481},{255,352},{128,97},{383,480},{256,225},{511,96},... | collective-permute-start | bytes 884744 | tf_op jit(solution)/shard_map/ppermute | solution.py:49
  11.3 1.3 %collective-permute-start.3 = (f32[104,768]{1,0:T(8,128)S(1)}, f32[104,768]{1,0:T(8,128)S(1)}, u32[]{:S(2)}, u32[]{:S(2)}) collective-permute-start(f32[104,768]{1,0:T(8,128)S(1)} %get-tuple-element.37), channel_id=1, source_target_pairs={{127,158},{0,415},{255,286},{128,31},{383,414},{256,159},{511,30},... | collective-permute-start | bytes 958472 | tf_op jit(solution)/shard_map/ppermute | solution.py:49
  12.6 0.0 collective-permute-done.9
  12.6 0.7 %collective-permute-start.7 = (f32[96,768]{1,0:T(8,128)S(1)}, f32[96,768]{1,0:T(8,128)S(1)}, u32[]{:S(2)}, u32[]{:S(2)}) collective-permute-start(f32[96,768]{1,0:T(8,128)S(1)} %get-tuple-element.39), channel_id=1, source_target_pairs={{127,222},{0,417},{255,350},{128,33},{383,478},{256,161},{511,94},... | collective-permute-start | bytes 884744 | tf_op jit(solution)/shard_map/ppermute | solution.py:49
  13.3 0.7 %collective-permute-start.10 = (f32[96,768]{1,0:T(8,128)S(1)}, f32[96,768]{1,0:T(8,128)S(1)}, u32[]{:S(2)}, u32[]{:S(2)}) collective-permute-start(f32[96,768]{1,0:T(8,128)S(1)} %collective-permute-done.9), channel_id=1, source_target_pairs={{124,0},{3,127},{252,128},{131,255},{380,256},{259,383},{508,384},... | collective-permute-start | bytes 884744 | tf_op jit(solution)/shard_map/ppermute | solution.py:59
  15.3 2.6 %shard_map.70 = (bf16[384,768]{1,0:T(8,128)(2,1)S(1)}, bf16[384,768]{1,0:T(8,128)(2,1)S(1)}, bf16[384,768]{1,0:T(8,128)(2,1)S(1)}, bf16[384,768]{1,0:T(8,128)(2,...) custom-call(f32[1]{0:T(128)S(6)} %copy.7.heat_ref, f32[1]{0:T(128)S(6)} %copy.8.bias_ref, ...), custom_call_target="tpu_custom_call" | custom-call | flops 1024 | bytes 1024 | tf_op jit(solution)/shard_map/pallas_call | solution.py:272
  17.9 3.1 %collective-permute-start.11 = (f32[384,768]{1,0:T(8,128)S(1)}, f32[384,768]{1,0:T(8,128)S(1)}, u32[]{:S(2)}, u32[]{:S(2)}) collective-permute-start(f32[384,768]{1,0:T(8,128)S(1)} %get-tuple-element.24.picture_ref), channel_id=1, source_target_pairs={{0,256},{1,257},{2,258},{3,259},{4,260},{5,261},{6,262},{7,263},{8... | collective-permute-start | bytes 3538952 | tf_op jit(solution)/shard_map/ppermute | solution.py:25
  21.1 3.4 %collective-permute-done.3 = f32[104,768]{1,0:T(8,128)S(1)} collective-permute-done((f32[104,768]{1,0:T(8,128)S(1)}, f32[104,768]{1,0:T(8,128)S(1)}, u32[]{:S(2)}, u32[]{:S(2)}) %collective-permute-start.3) | collective-permute-done | bytes 319520 | tf_op jit(solution)/shard_map/ppermute | solution.py:49
  24.5 1.9 %collective-permute-start = (f32[392,768]{1,0:T(8,128)S(1)}, f32[392,768]{1,0:T(8,128)S(1)}, u32[]{:S(2)}, u32[]{:S(2)}) collective-permute-start(f32[392,768]{1,0:T(8,128)S(1)} %get-tuple-element.31), channel_id=1, source_target_pairs={{0,1},{1,0},{2,3},{3,2},{4,5},{5,4},{6,7},{7,6},{8,9},{9,8},{10,11... | collective-permute-start | bytes 3612680 | tf_op jit(solution)/shard_map/ppermute | solution.py:25
  26.4 0.0 collective-permute-done.10.refs_3_
  26.4 0.7 %collective-permute-start.6 = (f32[96,768]{1,0:T(8,128)S(1)}, f32[96,768]{1,0:T(8,128)S(1)}, u32[]{:S(2)}, u32[]{:S(2)}) collective-permute-start(f32[96,768]{1,0:T(8,128)S(1)} %collective-permute-done.5), channel_id=1, source_target_pairs={{96,0},{97,127},{224,128},{225,255},{352,256},{353,383},{480,384},... | collective-permute-start | bytes 884744 | tf_op jit(solution)/shard_map/ppermute | solution.py:59
  27.1 11.9 %collective-permute-done.2.far_ref.tags_ref = f32[392,768]{1,0:T(8,128)S(1)} collective-permute-done((f32[392,768]{1,0:T(8,128)S(1)}, f32[392,768]{1,0:T(8,128)S(1)}, u32[]{:S(2)}, u32[]{:S(2)}) %collective-permute-start.2) | collective-permute-done | bytes 1204256 | tf_op jit(solution)/shard_map/ppermute | solution.py:25
  39.0 0.7 %collective-permute-start.8 = (f32[96,768]{1,0:T(8,128)S(1)}, f32[96,768]{1,0:T(8,128)S(1)}, u32[]{:S(2)}, u32[]{:S(2)}) collective-permute-start(f32[96,768]{1,0:T(8,128)S(1)} %collective-permute-done.7), channel_id=1, source_target_pairs={{94,0},{33,127},{222,128},{161,255},{350,256},{289,383},{478,384},... | collective-permute-start | bytes 884744 | tf_op jit(solution)/shard_map/ppermute | solution.py:59
  39.7 1.3 %collective-permute-start.4 = (f32[104,768]{1,0:T(8,128)S(1)}, f32[104,768]{1,0:T(8,128)S(1)}, u32[]{:S(2)}, u32[]{:S(2)}) collective-permute-start(f32[104,768]{1,0:T(8,128)S(1)} %collective-permute-done.3), channel_id=1, source_target_pairs={{30,0},{31,127},{158,128},{159,255},{286,256},{287,383},{414,384},... | collective-permute-start | bytes 958472 | tf_op jit(solution)/shard_map/ppermute | solution.py:59
  41.0 2.3 %shard_map.71.p_in_ref = f32[384,768]{1,0:T(8,128)S(1)} custom-call(f32[1]{0:T(128)S(6)} %copy.7.heat_ref, f32[1]{0:T(128)S(6)} %copy.8.bias_ref, f32[384,128]{1,0:T(8,128)S(1)} %get-tuple-element.23.own_tags_ref, bf16[384,768]{1,0:T(8,128)(2,1)S(1)} %get-tuple-element.29.high_ref.picture_high_ref, ...), custom_call_target="tpu_custom_call" | custom-call | flops 137438953472 | bytes 1024 | tf_op jit(solution)/shard_map/pallas_call | solution.py:272
  43.2 2.2 %shard_map.72 = (f32[384,768]{1,0:T(8,128)S(1)}, f32[384,768]{1,0:T(8,128)S(1)}) custom-call(f32[1]{0:T(128)S(6)} %copy.7.heat_ref, f32[1]{0:T(128)S(6)} %copy.8.bias_ref, f32[384,128]{1,0:T(8,128)S(1)} %get-tuple-element.23.own_tags_ref, bf16[384,768]{1,0:T(8,128)(2,1)S(1)} %get-tuple-element.27.caption_high_ref.high_ref, ...), custom_call_target="tpu_custom_call" | custom-call | flops 1024 | bytes 1024 | tf_op jit(solution)/shard_map/pallas_call | solution.py:272
  45.5 3.6 %shard_map.73 = (f32[384,768]{1,0:T(8,128)S(1)}, f32[384,768]{1,0:T(8,128)}) custom-call(f32[1]{0:T(128)S(6)} %copy.7.heat_ref, f32[1]{0:T(128)S(6)} %copy.8.bias_ref, f32[384,128]{1,0:T(8,128)S(1)} %get-tuple-element.23.own_tags_ref, f32[384,768]{1,0:T(8,128)S(1)} %get-tuple-element.24.picture_ref, f32[384,128]{1,0:T(8,128)S(1)} %get-tuple-element.25.scale_ref, ...), custom_call_target="tpu_custom_call" | custom-call | flops 1024 | bytes 1024 | tf_op jit(solution)/shard_map/pallas_call | solution.py:272
  49.1 14.0 %collective-permute-done.11.far_ref = f32[384,768]{1,0:T(8,128)S(1)} collective-permute-done((f32[384,768]{1,0:T(8,128)S(1)}, f32[384,768]{1,0:T(8,128)S(1)}, u32[]{:S(2)}, u32[]{:S(2)}) %collective-permute-start.11) | collective-permute-done | bytes 1179680 | tf_op jit(solution)/shard_map/ppermute | solution.py:25
  63.1 2.8 %shard_map.74 = f32[384,768]{1,0:T(8,128)} custom-call(f32[1]{0:T(128)S(6)} %copy.7.heat_ref, f32[1]{0:T(128)S(6)} %copy.8.bias_ref, f32[384,128]{1,0:T(8,128)S(1)} %get-tuple-element.23.own_tags_ref, f32[384,768]{1,0:T(8,128)S(1)} %get-tuple-element.26.caption_ref.unit_ref, f32[384,128]{1,0:T(8,128)S(1)} %get-tuple-element.42.scale_ref, ...), custom_call_target="tpu_custom_call" | custom-call | flops 1024 | bytes 1024 | tf_op jit(solution)/shard_map/pallas_call | solution.py:272
  (7 shorter events, 0.0 us)
Async XLA Ops:
  1.9 37.0 %collective-permute-start.2 = (f32[392,768]{1,0:T(8,128)S(1)}, f32[392,768]{1,0:T(8,128)S(1)}, u32[]{:S(2)}, u32[]{:S(2)}) collective-permute-start(f32[392,768]{1,0:T(8,128)S(1)} %shard_map.68.staged_ref), channel_id=1, source_target_pairs={{0,256},{1,257},{2,258},{3,259},{4,260},{5,261},{6,262},{7,263},{8... | collective-permute-start | bytes 3612680 | tf_op jit(solution)/shard_map/ppermute | solution.py:25
  7.8 31.8 %collective-permute-start.1 = (f32[392,768]{1,0:T(8,128)S(1)}, f32[392,768]{1,0:T(8,128)S(1)}, u32[]{:S(2)}, u32[]{:S(2)}) collective-permute-start(f32[392,768]{1,0:T(8,128)S(1)} %get-tuple-element.32), channel_id=1, source_target_pairs={{1,2},{2,1},{3,4},{4,3},{5,6},{6,5},{7,8},{8,7},{9,10},{10,9},{11,... | collective-permute-start | bytes 3612680 | tf_op jit(solution)/shard_map/ppermute | solution.py:25
  9.9 2.7 %collective-permute-start.9 = (f32[96,768]{1,0:T(8,128)S(1)}, f32[96,768]{1,0:T(8,128)S(1)}, u32[]{:S(2)}, u32[]{:S(2)}) collective-permute-start(f32[96,768]{1,0:T(8,128)S(1)} %get-tuple-element.40), channel_id=1, source_target_pairs={{127,252},{0,387},{255,380},{128,3},{383,508},{256,131},{511,124},... | collective-permute-start | bytes 884744 | tf_op jit(solution)/shard_map/ppermute | solution.py:49
  10.6 2.7 %collective-permute-start.5 = (f32[96,768]{1,0:T(8,128)S(1)}, f32[96,768]{1,0:T(8,128)S(1)}, u32[]{:S(2)}, u32[]{:S(2)}) collective-permute-start(f32[96,768]{1,0:T(8,128)S(1)} %get-tuple-element.38), channel_id=1, source_target_pairs={{127,224},{0,481},{255,352},{128,97},{383,480},{256,225},{511,96},... | collective-permute-start | bytes 884744 | tf_op jit(solution)/shard_map/ppermute | solution.py:49
  11.3 13.2 %collective-permute-start.3 = (f32[104,768]{1,0:T(8,128)S(1)}, f32[104,768]{1,0:T(8,128)S(1)}, u32[]{:S(2)}, u32[]{:S(2)}) collective-permute-start(f32[104,768]{1,0:T(8,128)S(1)} %get-tuple-element.37), channel_id=1, source_target_pairs={{127,158},{0,415},{255,286},{128,31},{383,414},{256,159},{511,30},... | collective-permute-start | bytes 958472 | tf_op jit(solution)/shard_map/ppermute | solution.py:49
  12.6 5.3 %collective-permute-start.7 = (f32[96,768]{1,0:T(8,128)S(1)}, f32[96,768]{1,0:T(8,128)S(1)}, u32[]{:S(2)}, u32[]{:S(2)}) collective-permute-start(f32[96,768]{1,0:T(8,128)S(1)} %get-tuple-element.39), channel_id=1, source_target_pairs={{127,222},{0,417},{255,350},{128,33},{383,478},{256,161},{511,94},... | collective-permute-start | bytes 884744 | tf_op jit(solution)/shard_map/ppermute | solution.py:49
  13.3 13.1 %collective-permute-start.10 = (f32[96,768]{1,0:T(8,128)S(1)}, f32[96,768]{1,0:T(8,128)S(1)}, u32[]{:S(2)}, u32[]{:S(2)}) collective-permute-start(f32[96,768]{1,0:T(8,128)S(1)} %collective-permute-done.9), channel_id=1, source_target_pairs={{124,0},{3,127},{252,128},{131,255},{380,256},{259,383},{508,384},... | collective-permute-start | bytes 884744 | tf_op jit(solution)/shard_map/ppermute | solution.py:59
  17.9 45.2 %collective-permute-start.11 = (f32[384,768]{1,0:T(8,128)S(1)}, f32[384,768]{1,0:T(8,128)S(1)}, u32[]{:S(2)}, u32[]{:S(2)}) collective-permute-start(f32[384,768]{1,0:T(8,128)S(1)} %get-tuple-element.24.picture_ref), channel_id=1, source_target_pairs={{0,256},{1,257},{2,258},{3,259},{4,260},{5,261},{6,262},{7,263},{8... | collective-permute-start | bytes 3538952 | tf_op jit(solution)/shard_map/ppermute | solution.py:25
  24.5 21.0 %collective-permute-start = (f32[392,768]{1,0:T(8,128)S(1)}, f32[392,768]{1,0:T(8,128)S(1)}, u32[]{:S(2)}, u32[]{:S(2)}) collective-permute-start(f32[392,768]{1,0:T(8,128)S(1)} %get-tuple-element.31), channel_id=1, source_target_pairs={{0,1},{1,0},{2,3},{3,2},{4,5},{5,4},{6,7},{7,6},{8,9},{9,8},{10,11... | collective-permute-start | bytes 3612680 | tf_op jit(solution)/shard_map/ppermute | solution.py:25
  26.4 19.1 %collective-permute-start.6 = (f32[96,768]{1,0:T(8,128)S(1)}, f32[96,768]{1,0:T(8,128)S(1)}, u32[]{:S(2)}, u32[]{:S(2)}) collective-permute-start(f32[96,768]{1,0:T(8,128)S(1)} %collective-permute-done.5), channel_id=1, source_target_pairs={{96,0},{97,127},{224,128},{225,255},{352,256},{353,383},{480,384},... | collective-permute-start | bytes 884744 | tf_op jit(solution)/shard_map/ppermute | solution.py:59
  39.0 6.5 %collective-permute-start.8 = (f32[96,768]{1,0:T(8,128)S(1)}, f32[96,768]{1,0:T(8,128)S(1)}, u32[]{:S(2)}, u32[]{:S(2)}) collective-permute-start(f32[96,768]{1,0:T(8,128)S(1)} %collective-permute-done.7), channel_id=1, source_target_pairs={{94,0},{33,127},{222,128},{161,255},{350,256},{289,383},{478,384},... | collective-permute-start | bytes 884744 | tf_op jit(solution)/shard_map/ppermute | solution.py:59
  39.7 5.8 %collective-permute-start.4 = (f32[104,768]{1,0:T(8,128)S(1)}, f32[104,768]{1,0:T(8,128)S(1)}, u32[]{:S(2)}, u32[]{:S(2)}) collective-permute-start(f32[104,768]{1,0:T(8,128)S(1)} %collective-permute-done.3), channel_id=1, source_target_pairs={{30,0},{31,127},{158,128},{159,255},{286,256},{287,383},{414,384},... | collective-permute-start | bytes 958472 | tf_op jit(solution)/shard_map/ppermute | solution.py:59

commit v5 on v4

--- a/solution.py
+++ b/solution.py
@@ -91,7 +91,9 @@
 
 def slopes(own, other, own_tags, other_tags, heat, bias):
     logit = heat * dot_nt(own, other) + bias
-    return 1.0 / (1.0 + jnp.exp(-logit)) - jnp.where(own_tags == other_tags, 1.0, 0.0)
+    same = own_tags == other_tags
+    slope = 1.0 / (1.0 + jnp.exp(jnp.where(same, logit, -logit)))
+    return jnp.where(same, -slope, slope)
 
 
 def pull(own, other, *tags_and_scalars):

time: 66.4 us -> 66.4 us (level)
  no operation moved by 1% of the time
where the time goes in v5:
time: 66.4 us; the launch traced here: 66 us
  waiting for transfers between devices  29.3 us (44%)
  starting transfers between devices  18 us (27%)
  Pallas kernels  16.6 us (25%)
  between operations  2.13 us (3%)
    ppermute x4, waiting for transfers between devices, swap(): lax.ppermute(block, 'dp', [pair for pair in route if pair[0] != pair[1]])  25.9 us
    pallas_call x5, Pallas kernels, call(): pl.pallas_call(kernel, out_shape=out_shape, in_specs=[SMEM if x.size == 1...  13.6 us
    ppermute x4, starting transfers between devices, swap(): lax.ppermute(block, 'dp', [pair for pair in route if pair[0] != pair[1]])  11.3 us
    ppermute x4, waiting for transfers between devices, outward(): return lax.ppermute(block, 'dp', route)  3.34 us
    ppermute x4, starting transfers between devices, homeward(): return lax.ppermute(block, 'dp', route)  3.34 us
    ppermute x4, starting transfers between devices, outward(): return lax.ppermute(block, 'dp', route)  3.33 us
    pallas_call x1, Pallas kernels, local(): pl.pallas_call(unit_kernel, out_shape=[f32(rows)] * 2 + [f32(rows + 8)] *...  1.69 us
  transfers between devices with their start and end apart: 12, of which 3 were waited for; matrix products, arithmetic and copies ran while one was open for 0% of the time, Pallas kernels for 19%

profile of v5, /device:TPU:488, one launch (start us, length us, event | category | flops | bytes accessed | tf_op | source)
XLA Modules:
  0.0 66.0 jit_solution(17821535115921449548)
XLA Ops:
  0.6 1.3 %shard_map.68.staged_ref = f32[392,768]{1,0:T(8,128)S(1)} custom-call(f32[384,768]{1,0:T(8,128)} %caption_ref.1, s32[384]{0:T(512)} %tags_ref.1), custom_call_target="tpu_custom_call" | custom-call | flops 1024 | bytes 1024 | tf_op jit(solution)/shard_map/pallas_call | solution.py:300
  1.9 4.2 %collective-permute-start.2 = (f32[392,768]{1,0:T(8,128)S(1)}, f32[392,768]{1,0:T(8,128)S(1)}, u32[]{:S(2)}, u32[]{:S(2)}) collective-permute-start(f32[392,768]{1,0:T(8,128)S(1)} %shard_map.68.staged_ref), channel_id=1, source_target_pairs={{0,256},{1,257},{2,258},{3,259},{4,260},{5,261},{6,262},{7,263},{8... | collective-permute-start | bytes 3612680 | tf_op jit(solution)/shard_map/ppermute | solution.py:25
  6.1 1.7 %shard_map.69 = (f32[384,768]{1,0:T(8,128)S(1)}, f32[384,768]{1,0:T(8,128)S(1)}, f32[392,768]{1,0:T(8,128)S(1)}, f32[392,768]{1,0:T(8,128)S(1)}, f32[384,128]{1,...) custom-call(f32[392,768]{1,0:T(8,128)S(1)} %shard_map.68.staged_ref,, ...), custom_call_target="tpu_custom_call" | custom-call | flops 1024 | bytes 1024 | tf_op jit(solution)/shard_map/pallas_call | solution.py:310
  7.8 2.1 %collective-permute-start.1 = (f32[392,768]{1,0:T(8,128)S(1)}, f32[392,768]{1,0:T(8,128)S(1)}, u32[]{:S(2)}, u32[]{:S(2)}) collective-permute-start(f32[392,768]{1,0:T(8,128)S(1)} %get-tuple-element.32), channel_id=1, source_target_pairs={{1,2},{2,1},{3,4},{4,3},{5,6},{6,5},{7,8},{8,7},{9,10},{10,9},{11,... | collective-permute-start | bytes 3612680 | tf_op jit(solution)/shard_map/ppermute | solution.py:25
  9.9 0.7 %collective-permute-start.9 = (f32[96,768]{1,0:T(8,128)S(1)}, f32[96,768]{1,0:T(8,128)S(1)}, u32[]{:S(2)}, u32[]{:S(2)}) collective-permute-start(f32[96,768]{1,0:T(8,128)S(1)} %get-tuple-element.40), channel_id=1, source_target_pairs={{127,252},{0,387},{255,380},{128,3},{383,508},{256,131},{511,124},... | collective-permute-start | bytes 884744 | tf_op jit(solution)/shard_map/ppermute | solution.py:49
  10.6 0.7 %collective-permute-start.5 = (f32[96,768]{1,0:T(8,128)S(1)}, f32[96,768]{1,0:T(8,128)S(1)}, u32[]{:S(2)}, u32[]{:S(2)}) collective-permute-start(f32[96,768]{1,0:T(8,128)S(1)} %get-tuple-element.38), channel_id=1, source_target_pairs={{127,224},{0,481},{255,352},{128,97},{383,480},{256,225},{511,96},... | collective-permute-start | bytes 884744 | tf_op jit(solution)/shard_map/ppermute | solution.py:49
  11.3 1.3 %collective-permute-start.3 = (f32[104,768]{1,0:T(8,128)S(1)}, f32[104,768]{1,0:T(8,128)S(1)}, u32[]{:S(2)}, u32[]{:S(2)}) collective-permute-start(f32[104,768]{1,0:T(8,128)S(1)} %get-tuple-element.37), channel_id=1, source_target_pairs={{127,158},{0,415},{255,286},{128,31},{383,414},{256,159},{511,30},... | collective-permute-start | bytes 958472 | tf_op jit(solution)/shard_map/ppermute | solution.py:49
  12.6 0.0 collective-permute-done.9
  12.6 0.7 %collective-permute-start.7 = (f32[96,768]{1,0:T(8,128)S(1)}, f32[96,768]{1,0:T(8,128)S(1)}, u32[]{:S(2)}, u32[]{:S(2)}) collective-permute-start(f32[96,768]{1,0:T(8,128)S(1)} %get-tuple-element.39), channel_id=1, source_target_pairs={{127,222},{0,417},{255,350},{128,33},{383,478},{256,161},{511,94},... | collective-permute-start | bytes 884744 | tf_op jit(solution)/shard_map/ppermute | solution.py:49
  13.3 0.7 %collective-permute-start.10 = (f32[96,768]{1,0:T(8,128)S(1)}, f32[96,768]{1,0:T(8,128)S(1)}, u32[]{:S(2)}, u32[]{:S(2)}) collective-permute-start(f32[96,768]{1,0:T(8,128)S(1)} %collective-permute-done.9), channel_id=1, source_target_pairs={{124,0},{3,127},{252,128},{131,255},{380,256},{259,383},{508,384},... | collective-permute-start | bytes 884744 | tf_op jit(solution)/shard_map/ppermute | solution.py:59
  15.3 2.7 %shard_map.70 = (bf16[384,768]{1,0:T(8,128)(2,1)S(1)}, bf16[384,768]{1,0:T(8,128)(2,1)S(1)}, bf16[384,768]{1,0:T(8,128)(2,1)S(1)}, bf16[384,768]{1,0:T(8,128)(2,...) custom-call(f32[1]{0:T(128)S(6)} %copy.7.heat_ref, f32[1]{0:T(128)S(6)} %copy.8.bias_ref, ...), custom_call_target="tpu_custom_call" | custom-call | flops 1024 | bytes 1024 | tf_op jit(solution)/shard_map/pallas_call | solution.py:274
  18.0 0.0 collective-permute-done.7
  18.0 3.1 %collective-permute-start.11 = (f32[384,768]{1,0:T(8,128)S(1)}, f32[384,768]{1,0:T(8,128)S(1)}, u32[]{:S(2)}, u32[]{:S(2)}) collective-permute-start(f32[384,768]{1,0:T(8,128)S(1)} %get-tuple-element.24.picture_ref), channel_id=1, source_target_pairs={{0,256},{1,257},{2,258},{3,259},{4,260},{5,261},{6,262},{7,263},{8... | collective-permute-start | bytes 3538952 | tf_op jit(solution)/shard_map/ppermute | solution.py:25
  21.1 3.3 %collective-permute-done.3 = f32[104,768]{1,0:T(8,128)S(1)} collective-permute-done((f32[104,768]{1,0:T(8,128)S(1)}, f32[104,768]{1,0:T(8,128)S(1)}, u32[]{:S(2)}, u32[]{:S(2)}) %collective-permute-start.3) | collective-permute-done | bytes 319520 | tf_op jit(solution)/shard_map/ppermute | solution.py:49
  24.5 1.9 %collective-permute-start = (f32[392,768]{1,0:T(8,128)S(1)}, f32[392,768]{1,0:T(8,128)S(1)}, u32[]{:S(2)}, u32[]{:S(2)}) collective-permute-start(f32[392,768]{1,0:T(8,128)S(1)} %get-tuple-element.31), channel_id=1, source_target_pairs={{0,1},{1,0},{2,3},{3,2},{4,5},{5,4},{6,7},{7,6},{8,9},{9,8},{10,11... | collective-permute-start | bytes 3612680 | tf_op jit(solution)/shard_map/ppermute | solution.py:25
  26.4 0.7 %collective-permute-start.6 = (f32[96,768]{1,0:T(8,128)S(1)}, f32[96,768]{1,0:T(8,128)S(1)}, u32[]{:S(2)}, u32[]{:S(2)}) collective-permute-start(f32[96,768]{1,0:T(8,128)S(1)} %collective-permute-done.5), channel_id=1, source_target_pairs={{96,0},{97,127},{224,128},{225,255},{352,256},{353,383},{480,384},... | collective-permute-start | bytes 884744 | tf_op jit(solution)/shard_map/ppermute | solution.py:59
  27.1 11.9 %collective-permute-done.2.far_ref.tags_ref = f32[392,768]{1,0:T(8,128)S(1)} collective-permute-done((f32[392,768]{1,0:T(8,128)S(1)}, f32[392,768]{1,0:T(8,128)S(1)}, u32[]{:S(2)}, u32[]{:S(2)}) %collective-permute-start.2) | collective-permute-done | bytes 1204256 | tf_op jit(solution)/shard_map/ppermute | solution.py:25
  39.0 0.7 %collective-permute-start.8 = (f32[96,768]{1,0:T(8,128)S(1)}, f32[96,768]{1,0:T(8,128)S(1)}, u32[]{:S(2)}, u32[]{:S(2)}) collective-permute-start(f32[96,768]{1,0:T(8,128)S(1)} %collective-permute-done.7), channel_id=1, source_target_pairs={{94,0},{33,127},{222,128},{161,255},{350,256},{289,383},{478,384},... | collective-permute-start | bytes 884744 | tf_op jit(solution)/shard_map/ppermute | solution.py:59
  39.7 1.3 %collective-permute-start.4 = (f32[104,768]{1,0:T(8,128)S(1)}, f32[104,768]{1,0:T(8,128)S(1)}, u32[]{:S(2)}, u32[]{:S(2)}) collective-permute-start(f32[104,768]{1,0:T(8,128)S(1)} %collective-permute-done.3), channel_id=1, source_target_pairs={{30,0},{31,127},{158,128},{159,255},{286,256},{287,383},{414,384},... | collective-permute-start | bytes 958472 | tf_op jit(solution)/shard_map/ppermute | solution.py:59
  41.0 2.3 %shard_map.71.p_in_ref = f32[384,768]{1,0:T(8,128)S(1)} custom-call(f32[1]{0:T(128)S(6)} %copy.7.heat_ref, f32[1]{0:T(128)S(6)} %copy.8.bias_ref, f32[384,128]{1,0:T(8,128)S(1)} %get-tuple-element.23.own_tags_ref, bf16[384,768]{1,0:T(8,128)(2,1)S(1)} %get-tuple-element.29.high_ref.picture_high_ref, ...), custom_call_target="tpu_custom_call" | custom-call | flops 137438953472 | bytes 1024 | tf_op jit(solution)/shard_map/pallas_call | solution.py:274
  43.2 2.2 %shard_map.72 = (f32[384,768]{1,0:T(8,128)S(1)}, f32[384,768]{1,0:T(8,128)S(1)}) custom-call(f32[1]{0:T(128)S(6)} %copy.7.heat_ref, f32[1]{0:T(128)S(6)} %copy.8.bias_ref, f32[384,128]{1,0:T(8,128)S(1)} %get-tuple-element.23.own_tags_ref, bf16[384,768]{1,0:T(8,128)(2,1)S(1)} %get-tuple-element.27.caption_high_ref.high_ref, ...), custom_call_target="tpu_custom_call" | custom-call | flops 1024 | bytes 1024 | tf_op jit(solution)/shard_map/pallas_call | solution.py:274
  45.5 3.6 %shard_map.73 = (f32[384,768]{1,0:T(8,128)S(1)}, f32[384,768]{1,0:T(8,128)}) custom-call(f32[1]{0:T(128)S(6)} %copy.7.heat_ref, f32[1]{0:T(128)S(6)} %copy.8.bias_ref, f32[384,128]{1,0:T(8,128)S(1)} %get-tuple-element.23.own_tags_ref, f32[384,768]{1,0:T(8,128)S(1)} %get-tuple-element.24.picture_ref, f32[384,128]{1,0:T(8,128)S(1)} %get-tuple-element.25.scale_ref, ...), custom_call_target="tpu_custom_call" | custom-call | flops 1024 | bytes 1024 | tf_op jit(solution)/shard_map/pallas_call | solution.py:274
  49.1 14.0 %collective-permute-done.11.far_ref = f32[384,768]{1,0:T(8,128)S(1)} collective-permute-done((f32[384,768]{1,0:T(8,128)S(1)}, f32[384,768]{1,0:T(8,128)S(1)}, u32[]{:S(2)}, u32[]{:S(2)}) %collective-permute-start.11) | collective-permute-done | bytes 1179680 | tf_op jit(solution)/shard_map/ppermute | solution.py:25
  63.1 2.9 %shard_map.74 = f32[384,768]{1,0:T(8,128)} custom-call(f32[1]{0:T(128)S(6)} %copy.7.heat_ref, f32[1]{0:T(128)S(6)} %copy.8.bias_ref, f32[384,128]{1,0:T(8,128)S(1)} %get-tuple-element.23.own_tags_ref, f32[384,768]{1,0:T(8,128)S(1)} %get-tuple-element.26.caption_ref.unit_ref, f32[384,128]{1,0:T(8,128)S(1)} %get-tuple-element.42.scale_ref, ...), custom_call_target="tpu_custom_call" | custom-call | flops 1024 | bytes 1024 | tf_op jit(solution)/shard_map/pallas_call | solution.py:274
  (7 shorter events, 0.0 us)
Async XLA Ops:
  1.9 37.0 %collective-permute-start.2 = (f32[392,768]{1,0:T(8,128)S(1)}, f32[392,768]{1,0:T(8,128)S(1)}, u32[]{:S(2)}, u32[]{:S(2)}) collective-permute-start(f32[392,768]{1,0:T(8,128)S(1)} %shard_map.68.staged_ref), channel_id=1, source_target_pairs={{0,256},{1,257},{2,258},{3,259},{4,260},{5,261},{6,262},{7,263},{8... | collective-permute-start | bytes 3612680 | tf_op jit(solution)/shard_map/ppermute | solution.py:25
  7.8 31.8 %collective-permute-start.1 = (f32[392,768]{1,0:T(8,128)S(1)}, f32[392,768]{1,0:T(8,128)S(1)}, u32[]{:S(2)}, u32[]{:S(2)}) collective-permute-start(f32[392,768]{1,0:T(8,128)S(1)} %get-tuple-element.32), channel_id=1, source_target_pairs={{1,2},{2,1},{3,4},{4,3},{5,6},{6,5},{7,8},{8,7},{9,10},{10,9},{11,... | collective-permute-start | bytes 3612680 | tf_op jit(solution)/shard_map/ppermute | solution.py:25
  9.9 2.7 %collective-permute-start.9 = (f32[96,768]{1,0:T(8,128)S(1)}, f32[96,768]{1,0:T(8,128)S(1)}, u32[]{:S(2)}, u32[]{:S(2)}) collective-permute-start(f32[96,768]{1,0:T(8,128)S(1)} %get-tuple-element.40), channel_id=1, source_target_pairs={{127,252},{0,387},{255,380},{128,3},{383,508},{256,131},{511,124},... | collective-permute-start | bytes 884744 | tf_op jit(solution)/shard_map/ppermute | solution.py:49
  10.6 2.7 %collective-permute-start.5 = (f32[96,768]{1,0:T(8,128)S(1)}, f32[96,768]{1,0:T(8,128)S(1)}, u32[]{:S(2)}, u32[]{:S(2)}) collective-permute-start(f32[96,768]{1,0:T(8,128)S(1)} %get-tuple-element.38), channel_id=1, source_target_pairs={{127,224},{0,481},{255,352},{128,97},{383,480},{256,225},{511,96},... | collective-permute-start | bytes 884744 | tf_op jit(solution)/shard_map/ppermute | solution.py:49
  11.3 13.2 %collective-permute-start.3 = (f32[104,768]{1,0:T(8,128)S(1)}, f32[104,768]{1,0:T(8,128)S(1)}, u32[]{:S(2)}, u32[]{:S(2)}) collective-permute-start(f32[104,768]{1,0:T(8,128)S(1)} %get-tuple-element.37), channel_id=1, source_target_pairs={{127,158},{0,415},{255,286},{128,31},{383,414},{256,159},{511,30},... | collective-permute-start | bytes 958472 | tf_op jit(solution)/shard_map/ppermute | solution.py:49
  12.6 5.4 %collective-permute-start.7 = (f32[96,768]{1,0:T(8,128)S(1)}, f32[96,768]{1,0:T(8,128)S(1)}, u32[]{:S(2)}, u32[]{:S(2)}) collective-permute-start(f32[96,768]{1,0:T(8,128)S(1)} %get-tuple-element.39), channel_id=1, source_target_pairs={{127,222},{0,417},{255,350},{128,33},{383,478},{256,161},{511,94},... | collective-permute-start | bytes 884744 | tf_op jit(solution)/shard_map/ppermute | solution.py:49
  13.3 13.1 %collective-permute-start.10 = (f32[96,768]{1,0:T(8,128)S(1)}, f32[96,768]{1,0:T(8,128)S(1)}, u32[]{:S(2)}, u32[]{:S(2)}) collective-permute-start(f32[96,768]{1,0:T(8,128)S(1)} %collective-permute-done.9), channel_id=1, source_target_pairs={{124,0},{3,127},{252,128},{131,255},{380,256},{259,383},{508,384},... | collective-permute-start | bytes 884744 | tf_op jit(solution)/shard_map/ppermute | solution.py:59
  18.0 45.1 %collective-permute-start.11 = (f32[384,768]{1,0:T(8,128)S(1)}, f32[384,768]{1,0:T(8,128)S(1)}, u32[]{:S(2)}, u32[]{:S(2)}) collective-permute-start(f32[384,768]{1,0:T(8,128)S(1)} %get-tuple-element.24.picture_ref), channel_id=1, source_target_pairs={{0,256},{1,257},{2,258},{3,259},{4,260},{5,261},{6,262},{7,263},{8... | collective-permute-start | bytes 3538952 | tf_op jit(solution)/shard_map/ppermute | solution.py:25
  24.5 21.0 %collective-permute-start = (f32[392,768]{1,0:T(8,128)S(1)}, f32[392,768]{1,0:T(8,128)S(1)}, u32[]{:S(2)}, u32[]{:S(2)}) collective-permute-start(f32[392,768]{1,0:T(8,128)S(1)} %get-tuple-element.31), channel_id=1, source_target_pairs={{0,1},{1,0},{2,3},{3,2},{4,5},{5,4},{6,7},{7,6},{8,9},{9,8},{10,11... | collective-permute-start | bytes 3612680 | tf_op jit(solution)/shard_map/ppermute | solution.py:25
  26.4 19.1 %collective-permute-start.6 = (f32[96,768]{1,0:T(8,128)S(1)}, f32[96,768]{1,0:T(8,128)S(1)}, u32[]{:S(2)}, u32[]{:S(2)}) collective-permute-start(f32[96,768]{1,0:T(8,128)S(1)} %collective-permute-done.5), channel_id=1, source_target_pairs={{96,0},{97,127},{224,128},{225,255},{352,256},{353,383},{480,384},... | collective-permute-start | bytes 884744 | tf_op jit(solution)/shard_map/ppermute | solution.py:59
  39.0 6.5 %collective-permute-start.8 = (f32[96,768]{1,0:T(8,128)S(1)}, f32[96,768]{1,0:T(8,128)S(1)}, u32[]{:S(2)}, u32[]{:S(2)}) collective-permute-start(f32[96,768]{1,0:T(8,128)S(1)} %collective-permute-done.7), channel_id=1, source_target_pairs={{94,0},{33,127},{222,128},{161,255},{350,256},{289,383},{478,384},... | collective-permute-start | bytes 884744 | tf_op jit(solution)/shard_map/ppermute | solution.py:59
  39.7 5.8 %collective-permute-start.4 = (f32[104,768]{1,0:T(8,128)S(1)}, f32[104,768]{1,0:T(8,128)S(1)}, u32[]{:S(2)}, u32[]{:S(2)}) collective-permute-start(f32[104,768]{1,0:T(8,128)S(1)} %collective-permute-done.3), channel_id=1, source_target_pairs={{30,0},{31,127},{158,128},{159,255},{286,256},{287,383},{414,384},... | collective-permute-start | bytes 958472 | tf_op jit(solution)/shard_map/ppermute | solution.py:59

commit v6 on v5

--- a/solution.py
+++ b/solution.py
@@ -9,9 +9,10 @@
 NN = (((1,), (0,)), ((), ()))
 PLANE = 128
 DEEP = 16
-UP_BY = ((0, 15), (3, 0), (2, 15), (3, 14))
-DOWN_BY = ((0, 15), (3, 0), (1, 0), (0, 1))
-PARTS = len(UP_BY)
+UP_BY = ((0, 15), (3, 0), (2, 15))
+DOWN_BY = ((0, 15), (3, 0), (1, 0))
+ENDS = (0, 96, 192, 288, 384)
+PARTS = len(ENDS) - 1
 BLOCKS = 3
 STAGES = 4
 FAR_COST = 1 << 37
@@ -41,7 +42,7 @@
 
 def outward(block, k):
     count = lax.axis_size("dp")
-    up, down = relays(k)
+    up, down = relays(k) if k < len(UP_BY) else (0, PLANE - 1)
     route = []
     for plane in range(0, count, PLANE):
         route.append((plane + PLANE - 1, (plane + PLANE) % count + up))
@@ -162,9 +163,8 @@
     chip = jnp.where(even, picture, caption)
     chip_out[:rows, :] = chip
     put_tags(chip_out, tags)
-    step = rows // PARTS
     for k, part in enumerate(parts):
-        part[:step, :] = chip[k * step : (k + 1) * step, :]
+        part[: ENDS[k + 1] - ENDS[k], :] = chip[ENDS[k] : ENDS[k + 1], :]
     put_tags(parts[0], tags)
 
 
@@ -229,7 +229,6 @@
     parts, (c_ref, p_ref, block) = refs[:PARTS], refs[PARTS:]
     heat, bias = scalars(heat_ref, bias_ref)
     rows = c_ref.shape[0]
-    step = rows // PARTS
     even = is_even()
     caption, picture = (caption_high_ref, caption_low_ref), (picture_high_ref, picture_low_ref)
     more = near_pull(heat, bias, own_tags_ref, caption, picture, even, other_ref)
@@ -239,8 +238,8 @@
     @pl.when(in_parts(place_in_plane()))
     def _():
         for k, part in enumerate(parts):
-            block[k * step : (k + 1) * step, :] = part[:step, :]
-        block[rows:, :] = parts[0][step:, :]
+            block[ENDS[k] : ENDS[k + 1], :] = part[: ENDS[k + 1] - ENDS[k], :]
+        block[rows:, :] = parts[0][ENDS[1] :, :]
         more = near_pull(heat, bias, own_tags_ref, caption, picture, jnp.logical_not(even), block)
         c_ref[...] += jnp.where(even, 0.0, more)
         p_ref[...] += jnp.where(even, more, 0.0)
@@ -285,7 +284,6 @@
 def local(picture, caption, tags, heat, bias):
     count = lax.axis_size("dp")
     rows, width = picture.shape
-    step = rows // PARTS
 
     def f32(n, m=width):
         return jax.ShapeDtypeStruct((n, m), jnp.float32)
@@ -310,7 +308,7 @@
     caption, picture, core, chip, own_tags, caption_scale, picture_scale, *parts = pl.pallas_call(
         unit_kernel,
         out_shape=[f32(rows)] * 2 + [f32(rows + 8)] * 2 + [f32(rows, 128)] * 3
-        + [f32(step + 8)] + [f32(step)] * (PARTS - 1),
+        + [f32(ENDS[1] + 8)] + [f32(ENDS[k + 1] - ENDS[k]) for k in range(1, PARTS)],
         in_specs=[VMEM, hbm],
         out_specs=[VMEM] * (7 + PARTS),
         scratch_shapes=[pltpu.VMEM((rows, width), jnp.float32), pltpu.SemaphoreType.DMA(())],
@@ -318,7 +316,7 @@
         compiler_params=pltpu.CompilerParams(vmem_limit_bytes=24 * 1024 * 1024),
     )(staged, pltpu.with_memory_space_constraint(picture, pltpu.HBM))
     parts = [outward(part, k) for k, part in enumerate(parts)]
-    parts = [homeward(part, k) for k, part in enumerate(parts)]
+    parts[:-1] = [homeward(part, k) for k, part in enumerate(parts[:-1])]
     core = swap(core, over_core)
     chip = swap(chip, over_chip)
     far_picture = swap(picture, over_half)

time: 66.4 us -> 66.4 us (level)
  starting transfers between devices: 18 us -> 17.3 us
  waiting for transfers between devices: 29.3 us -> 30 us
    ppermute x4, waiting for transfers between devices: 25.9 us -> 28.5 us  [swap(): lax.ppermute(block, 'dp', [pair for pair in route if pair[0] != pair[1]])]
    ppermute x4, waiting for transfers between devices: 3.34 us -> 1.41 us  [outward(): return lax.ppermute(block, 'dp', route)]
    ppermute x4 -> x3, starting transfers between devices: 3.34 us -> 2.65 us  [homeward(): return lax.ppermute(block, 'dp', route)]
  transfers between devices with their start and end apart: 12 -> 11, of which waited for: 3 -> 3; matrix products, arithmetic and copies ran while one was open for 0% -> 0% of each run, Pallas kernels for 19% -> 19%
where the time goes in v6:
time: 66.4 us; the launch traced here: 66 us
  waiting for transfers between devices  30 us (45%)
  starting transfers between devices  17.3 us (26%)
  Pallas kernels  16.6 us (25%)
  between operations  2.12 us (3%)
    ppermute x4, waiting for transfers between devices, swap(): lax.ppermute(block, 'dp', [pair for pair in route if pair[0] != pair[1]])  28.5 us
    pallas_call x5, Pallas kernels, call(): pl.pallas_call(kernel, out_shape=out_shape, in_specs=[SMEM if x.size == 1...  13.6 us
    ppermute x4, starting transfers between devices, swap(): lax.ppermute(block, 'dp', [pair for pair in route if pair[0] != pair[1]])  11.3 us
    ppermute x4, starting transfers between devices, outward(): return lax.ppermute(block, 'dp', route)  3.33 us
    ppermute x3, starting transfers between devices, homeward(): return lax.ppermute(block, 'dp', route)  2.65 us
    pallas_call x1, Pallas kernels, local(): pl.pallas_call(unit_kernel, out_shape=[f32(rows)] * 2 + [f32(rows + 8)] *...  1.69 us
    ppermute x4, waiting for transfers between devices, outward(): return lax.ppermute(block, 'dp', route)  1.41 us
  transfers between devices with their start and end apart: 11, of which 3 were waited for; matrix products, arithmetic and copies ran while one was open for 0% of the time, Pallas kernels for 19%

profile of v6, /device:TPU:488, one launch (start us, length us, event | category | flops | bytes accessed | tf_op | source)
XLA Modules:
  0.0 66.0 jit_solution(749352238126709468)
XLA Ops:
  0.6 1.3 %shard_map.68.staged_ref = f32[392,768]{1,0:T(8,128)S(1)} custom-call(f32[384,768]{1,0:T(8,128)} %caption_ref.1, s32[384]{0:T(512)} %tags_ref.1), custom_call_target="tpu_custom_call" | custom-call | flops 1024 | bytes 1024 | tf_op jit(solution)/shard_map/pallas_call | solution.py:298
  1.9 4.2 %collective-permute-start.2 = (f32[392,768]{1,0:T(8,128)S(1)}, f32[392,768]{1,0:T(8,128)S(1)}, u32[]{:S(2)}, u32[]{:S(2)}) collective-permute-start(f32[392,768]{1,0:T(8,128)S(1)} %shard_map.68.staged_ref), channel_id=1, source_target_pairs={{0,256},{1,257},{2,258},{3,259},{4,260},{5,261},{6,262},{7,263},{8... | collective-permute-start | bytes 3612680 | tf_op jit(solution)/shard_map/ppermute | solution.py:26
  6.1 1.7 %shard_map.69 = (f32[384,768]{1,0:T(8,128)S(1)}, f32[384,768]{1,0:T(8,128)S(1)}, f32[392,768]{1,0:T(8,128)S(1)}, f32[392,768]{1,0:T(8,128)S(1)}, f32[384,128]{1,...) custom-call(f32[392,768]{1,0:T(8,128)S(1)} %shard_map.68.staged_ref,, ...), custom_call_target="tpu_custom_call" | custom-call | flops 1024 | bytes 1024 | tf_op jit(solution)/shard_map/pallas_call | solution.py:308
  7.8 2.1 %collective-permute-start.1 = (f32[392,768]{1,0:T(8,128)S(1)}, f32[392,768]{1,0:T(8,128)S(1)}, u32[]{:S(2)}, u32[]{:S(2)}) collective-permute-start(f32[392,768]{1,0:T(8,128)S(1)} %get-tuple-element.32), channel_id=1, source_target_pairs={{1,2},{2,1},{3,4},{4,3},{5,6},{6,5},{7,8},{8,7},{9,10},{10,9},{11,... | collective-permute-start | bytes 3612680 | tf_op jit(solution)/shard_map/ppermute | solution.py:26
  9.9 0.7 %collective-permute-start.5 = (f32[96,768]{1,0:T(8,128)S(1)}, f32[96,768]{1,0:T(8,128)S(1)}, u32[]{:S(2)}, u32[]{:S(2)}) collective-permute-start(f32[96,768]{1,0:T(8,128)S(1)} %get-tuple-element.38), channel_id=1, source_target_pairs={{127,224},{0,481},{255,352},{128,97},{383,480},{256,225},{511,96},... | collective-permute-start | bytes 884744 | tf_op jit(solution)/shard_map/ppermute | solution.py:50
  10.6 1.3 %collective-permute-start.3 = (f32[104,768]{1,0:T(8,128)S(1)}, f32[104,768]{1,0:T(8,128)S(1)}, u32[]{:S(2)}, u32[]{:S(2)}) collective-permute-start(f32[104,768]{1,0:T(8,128)S(1)} %get-tuple-element.37), channel_id=1, source_target_pairs={{127,158},{0,415},{255,286},{128,31},{383,414},{256,159},{511,30},... | collective-permute-start | bytes 958472 | tf_op jit(solution)/shard_map/ppermute | solution.py:50
  11.9 0.7 %collective-permute-start.7 = (f32[96,768]{1,0:T(8,128)S(1)}, f32[96,768]{1,0:T(8,128)S(1)}, u32[]{:S(2)}, u32[]{:S(2)}) collective-permute-start(f32[96,768]{1,0:T(8,128)S(1)} %get-tuple-element.39), channel_id=1, source_target_pairs={{127,222},{0,417},{255,350},{128,33},{383,478},{256,161},{511,94},... | collective-permute-start | bytes 884744 | tf_op jit(solution)/shard_map/ppermute | solution.py:50
  12.6 0.0 collective-permute-done.5
  12.6 0.7 %collective-permute-start.9 = (f32[96,768]{1,0:T(8,128)S(1)}, f32[96,768]{1,0:T(8,128)S(1)}, u32[]{:S(2)}, u32[]{:S(2)}) collective-permute-start(f32[96,768]{1,0:T(8,128)S(1)} %get-tuple-element.40), channel_id=1, source_target_pairs={{127,128},{0,511},{255,256},{128,127},{383,384},{256,255},{511,0},... | collective-permute-start | bytes 884744 | tf_op jit(solution)/shard_map/ppermute | solution.py:50
  14.6 2.7 %shard_map.70 = (bf16[384,768]{1,0:T(8,128)(2,1)S(1)}, bf16[384,768]{1,0:T(8,128)(2,1)S(1)}, bf16[384,768]{1,0:T(8,128)(2,1)S(1)}, bf16[384,768]{1,0:T(8,128)(2,...) custom-call(f32[1]{0:T(128)S(6)} %copy.7.heat_ref, f32[1]{0:T(128)S(6)} %copy.8.bias_ref, ...), custom_call_target="tpu_custom_call" | custom-call | flops 1024 | bytes 1024 | tf_op jit(solution)/shard_map/pallas_call | solution.py:273
  17.3 0.0 collective-permute-done.7
  17.3 3.1 %collective-permute-start.10 = (f32[384,768]{1,0:T(8,128)S(1)}, f32[384,768]{1,0:T(8,128)S(1)}, u32[]{:S(2)}, u32[]{:S(2)}) collective-permute-start(f32[384,768]{1,0:T(8,128)S(1)} %get-tuple-element.24.picture_ref), channel_id=1, source_target_pairs={{0,256},{1,257},{2,258},{3,259},{4,260},{5,261},{6,262},{7,263},{8... | collective-permute-start | bytes 3538952 | tf_op jit(solution)/shard_map/ppermute | solution.py:26
  20.4 1.9 %collective-permute-start = (f32[392,768]{1,0:T(8,128)S(1)}, f32[392,768]{1,0:T(8,128)S(1)}, u32[]{:S(2)}, u32[]{:S(2)}) collective-permute-start(f32[392,768]{1,0:T(8,128)S(1)} %get-tuple-element.31), channel_id=1, source_target_pairs={{0,1},{1,0},{2,3},{3,2},{4,5},{5,4},{6,7},{7,6},{8,9},{9,8},{10,11... | collective-permute-start | bytes 3612680 | tf_op jit(solution)/shard_map/ppermute | solution.py:26
  22.4 1.4 %collective-permute-done.3 = f32[104,768]{1,0:T(8,128)S(1)} collective-permute-done((f32[104,768]{1,0:T(8,128)S(1)}, f32[104,768]{1,0:T(8,128)S(1)}, u32[]{:S(2)}, u32[]{:S(2)}) %collective-permute-start.3) | collective-permute-done | bytes 319520 | tf_op jit(solution)/shard_map/ppermute | solution.py:50
  23.8 0.7 %collective-permute-start.6 = (f32[96,768]{1,0:T(8,128)S(1)}, f32[96,768]{1,0:T(8,128)S(1)}, u32[]{:S(2)}, u32[]{:S(2)}) collective-permute-start(f32[96,768]{1,0:T(8,128)S(1)} %collective-permute-done.5), channel_id=1, source_target_pairs={{96,0},{97,127},{224,128},{225,255},{352,256},{353,383},{480,384},... | collective-permute-start | bytes 884744 | tf_op jit(solution)/shard_map/ppermute | solution.py:60
  24.4 14.5 %collective-permute-done.2.far_ref.tags_ref = f32[392,768]{1,0:T(8,128)S(1)} collective-permute-done((f32[392,768]{1,0:T(8,128)S(1)}, f32[392,768]{1,0:T(8,128)S(1)}, u32[]{:S(2)}, u32[]{:S(2)}) %collective-permute-start.2) | collective-permute-done | bytes 1204256 | tf_op jit(solution)/shard_map/ppermute | solution.py:26
  39.0 0.7 %collective-permute-start.8 = (f32[96,768]{1,0:T(8,128)S(1)}, f32[96,768]{1,0:T(8,128)S(1)}, u32[]{:S(2)}, u32[]{:S(2)}) collective-permute-start(f32[96,768]{1,0:T(8,128)S(1)} %collective-permute-done.7), channel_id=1, source_target_pairs={{94,0},{33,127},{222,128},{161,255},{350,256},{289,383},{478,384},... | collective-permute-start | bytes 884744 | tf_op jit(solution)/shard_map/ppermute | solution.py:60
  39.7 1.3 %collective-permute-start.4 = (f32[104,768]{1,0:T(8,128)S(1)}, f32[104,768]{1,0:T(8,128)S(1)}, u32[]{:S(2)}, u32[]{:S(2)}) collective-permute-start(f32[104,768]{1,0:T(8,128)S(1)} %collective-permute-done.3), channel_id=1, source_target_pairs={{30,0},{31,127},{158,128},{159,255},{286,256},{287,383},{414,384},... | collective-permute-start | bytes 958472 | tf_op jit(solution)/shard_map/ppermute | solution.py:60
  41.0 2.3 %shard_map.71.p_in_ref = f32[384,768]{1,0:T(8,128)S(1)} custom-call(f32[1]{0:T(128)S(6)} %copy.7.heat_ref, f32[1]{0:T(128)S(6)} %copy.8.bias_ref, f32[384,128]{1,0:T(8,128)S(1)} %get-tuple-element.23.own_tags_ref, bf16[384,768]{1,0:T(8,128)(2,1)S(1)} %get-tuple-element.29.high_ref.picture_high_ref, ...), custom_call_target="tpu_custom_call" | custom-call | flops 137438953472 | bytes 1024 | tf_op jit(solution)/shard_map/pallas_call | solution.py:273
  43.2 2.2 %shard_map.72 = (f32[384,768]{1,0:T(8,128)S(1)}, f32[384,768]{1,0:T(8,128)S(1)}) custom-call(f32[1]{0:T(128)S(6)} %copy.7.heat_ref, f32[1]{0:T(128)S(6)} %copy.8.bias_ref, f32[384,128]{1,0:T(8,128)S(1)} %get-tuple-element.23.own_tags_ref, bf16[384,768]{1,0:T(8,128)(2,1)S(1)} %get-tuple-element.27.caption_high_ref.high_ref, ...), custom_call_target="tpu_custom_call" | custom-call | flops 1024 | bytes 1024 | tf_op jit(solution)/shard_map/pallas_call | solution.py:273
  45.5 0.0 collective-permute-done.4.refs_0_
  45.5 3.6 %shard_map.73 = (f32[384,768]{1,0:T(8,128)S(1)}, f32[384,768]{1,0:T(8,128)}) custom-call(f32[1]{0:T(128)S(6)} %copy.7.heat_ref, f32[1]{0:T(128)S(6)} %copy.8.bias_ref, f32[384,128]{1,0:T(8,128)S(1)} %get-tuple-element.23.own_tags_ref, f32[384,768]{1,0:T(8,128)S(1)} %get-tuple-element.24.picture_ref, f32[384,128]{1,0:T(8,128)S(1)} %get-tuple-element.25.scale_ref, ...), custom_call_target="tpu_custom_call" | custom-call | flops 1024 | bytes 1024 | tf_op jit(solution)/shard_map/pallas_call | solution.py:273
  49.1 14.0 %collective-permute-done.10.far_ref = f32[384,768]{1,0:T(8,128)S(1)} collective-permute-done((f32[384,768]{1,0:T(8,128)S(1)}, f32[384,768]{1,0:T(8,128)S(1)}, u32[]{:S(2)}, u32[]{:S(2)}) %collective-permute-start.10) | collective-permute-done | bytes 1179680 | tf_op jit(solution)/shard_map/ppermute | solution.py:26
  63.1 2.9 %shard_map.74 = f32[384,768]{1,0:T(8,128)} custom-call(f32[1]{0:T(128)S(6)} %copy.7.heat_ref, f32[1]{0:T(128)S(6)} %copy.8.bias_ref, f32[384,128]{1,0:T(8,128)S(1)} %get-tuple-element.23.own_tags_ref, f32[384,768]{1,0:T(8,128)S(1)} %get-tuple-element.26.caption_ref.unit_ref, f32[384,128]{1,0:T(8,128)S(1)} %get-tuple-element.42.scale_ref, ...), custom_call_target="tpu_custom_call" | custom-call | flops 1024 | bytes 1024 | tf_op jit(solution)/shard_map/pallas_call | solution.py:273
  (5 shorter events, 0.0 us)
Async XLA Ops:
  1.9 37.0 %collective-permute-start.2 = (f32[392,768]{1,0:T(8,128)S(1)}, f32[392,768]{1,0:T(8,128)S(1)}, u32[]{:S(2)}, u32[]{:S(2)}) collective-permute-start(f32[392,768]{1,0:T(8,128)S(1)} %shard_map.68.staged_ref), channel_id=1, source_target_pairs={{0,256},{1,257},{2,258},{3,259},{4,260},{5,261},{6,262},{7,263},{8... | collective-permute-start | bytes 3612680 | tf_op jit(solution)/shard_map/ppermute | solution.py:26
  7.8 31.8 %collective-permute-start.1 = (f32[392,768]{1,0:T(8,128)S(1)}, f32[392,768]{1,0:T(8,128)S(1)}, u32[]{:S(2)}, u32[]{:S(2)}) collective-permute-start(f32[392,768]{1,0:T(8,128)S(1)} %get-tuple-element.32), channel_id=1, source_target_pairs={{1,2},{2,1},{3,4},{4,3},{5,6},{6,5},{7,8},{8,7},{9,10},{10,9},{11,... | collective-permute-start | bytes 3612680 | tf_op jit(solution)/shard_map/ppermute | solution.py:26
  9.9 2.7 %collective-permute-start.5 = (f32[96,768]{1,0:T(8,128)S(1)}, f32[96,768]{1,0:T(8,128)S(1)}, u32[]{:S(2)}, u32[]{:S(2)}) collective-permute-start(f32[96,768]{1,0:T(8,128)S(1)} %get-tuple-element.38), channel_id=1, source_target_pairs={{127,224},{0,481},{255,352},{128,97},{383,480},{256,225},{511,96},... | collective-permute-start | bytes 884744 | tf_op jit(solution)/shard_map/ppermute | solution.py:50
  10.6 13.2 %collective-permute-start.3 = (f32[104,768]{1,0:T(8,128)S(1)}, f32[104,768]{1,0:T(8,128)S(1)}, u32[]{:S(2)}, u32[]{:S(2)}) collective-permute-start(f32[104,768]{1,0:T(8,128)S(1)} %get-tuple-element.37), channel_id=1, source_target_pairs={{127,158},{0,415},{255,286},{128,31},{383,414},{256,159},{511,30},... | collective-permute-start | bytes 958472 | tf_op jit(solution)/shard_map/ppermute | solution.py:50
  11.9 5.4 %collective-permute-start.7 = (f32[96,768]{1,0:T(8,128)S(1)}, f32[96,768]{1,0:T(8,128)S(1)}, u32[]{:S(2)}, u32[]{:S(2)}) collective-permute-start(f32[96,768]{1,0:T(8,128)S(1)} %get-tuple-element.39), channel_id=1, source_target_pairs={{127,222},{0,417},{255,350},{128,33},{383,478},{256,161},{511,94},... | collective-permute-start | bytes 884744 | tf_op jit(solution)/shard_map/ppermute | solution.py:50
  12.6 7.8 %collective-permute-start.9 = (f32[96,768]{1,0:T(8,128)S(1)}, f32[96,768]{1,0:T(8,128)S(1)}, u32[]{:S(2)}, u32[]{:S(2)}) collective-permute-start(f32[96,768]{1,0:T(8,128)S(1)} %get-tuple-element.40), channel_id=1, source_target_pairs={{127,128},{0,511},{255,256},{128,127},{383,384},{256,255},{511,0},... | collective-permute-start | bytes 884744 | tf_op jit(solution)/shard_map/ppermute | solution.py:50
  17.3 45.8 %collective-permute-start.10 = (f32[384,768]{1,0:T(8,128)S(1)}, f32[384,768]{1,0:T(8,128)S(1)}, u32[]{:S(2)}, u32[]{:S(2)}) collective-permute-start(f32[384,768]{1,0:T(8,128)S(1)} %get-tuple-element.24.picture_ref), channel_id=1, source_target_pairs={{0,256},{1,257},{2,258},{3,259},{4,260},{5,261},{6,262},{7,263},{8... | collective-permute-start | bytes 3538952 | tf_op jit(solution)/shard_map/ppermute | solution.py:26
  20.4 25.1 %collective-permute-start = (f32[392,768]{1,0:T(8,128)S(1)}, f32[392,768]{1,0:T(8,128)S(1)}, u32[]{:S(2)}, u32[]{:S(2)}) collective-permute-start(f32[392,768]{1,0:T(8,128)S(1)} %get-tuple-element.31), channel_id=1, source_target_pairs={{0,1},{1,0},{2,3},{3,2},{4,5},{5,4},{6,7},{7,6},{8,9},{9,8},{10,11... | collective-permute-start | bytes 3612680 | tf_op jit(solution)/shard_map/ppermute | solution.py:26
  23.8 21.7 %collective-permute-start.6 = (f32[96,768]{1,0:T(8,128)S(1)}, f32[96,768]{1,0:T(8,128)S(1)}, u32[]{:S(2)}, u32[]{:S(2)}) collective-permute-start(f32[96,768]{1,0:T(8,128)S(1)} %collective-permute-done.5), channel_id=1, source_target_pairs={{96,0},{97,127},{224,128},{225,255},{352,256},{353,383},{480,384},... | collective-permute-start | bytes 884744 | tf_op jit(solution)/shard_map/ppermute | solution.py:60
  39.0 6.5 %collective-permute-start.8 = (f32[96,768]{1,0:T(8,128)S(1)}, f32[96,768]{1,0:T(8,128)S(1)}, u32[]{:S(2)}, u32[]{:S(2)}) collective-permute-start(f32[96,768]{1,0:T(8,128)S(1)} %collective-permute-done.7), channel_id=1, source_target_pairs={{94,0},{33,127},{222,128},{161,255},{350,256},{289,383},{478,384},... | collective-permute-start | bytes 884744 | tf_op jit(solution)/shard_map/ppermute | solution.py:60
  39.7 5.8 %collective-permute-start.4 = (f32[104,768]{1,0:T(8,128)S(1)}, f32[104,768]{1,0:T(8,128)S(1)}, u32[]{:S(2)}, u32[]{:S(2)}) collective-permute-start(f32[104,768]{1,0:T(8,128)S(1)} %collective-permute-done.3), channel_id=1, source_target_pairs={{30,0},{31,127},{158,128},{159,255},{286,256},{287,383},{414,384},... | collective-permute-start | bytes 958472 | tf_op jit(solution)/shard_map/ppermute | solution.py:60
